TPU v7x, 128 devices: a whole 4x4x4 slice. The times are simulated.
128 devices in a mesh: gx: 16 (over x, y), gy: 8 (over z, core).
Axes of the slice: x: 4, y: 4, z: 4, core: 2. Of those that a mesh axis runs over, the one named last changes fastest.
Arguments:
- state: float32 [512, 256, 2048], P('gx', 'gy'), may hold values from 0.1 to 4
- lat_coef: float32 [512, 256], P('gx', 'gy'), may hold values from 0.05 to 0.2
- diffusion: float32 [512, 256, 64], P('gx', 'gy'), may hold values from 0.05 to 1
- layer_count: int32 [512, 256], P('gx', 'gy'), may hold values from 32 to 64
- species_scale: float32 [32], replicated, may hold values from 0.1 to 10
- stream: float32 [524288, 32], P(('gx', 'gy')), may hold values from 0.1 to 4
- reach_owner: int32 [524288, 1], P(('gx', 'gy')), may hold values from 0 to 127; in each aligned block of 4096 rows (0 to 4095, 4096 to 8191, ...) at most 64 rows name the same one
- reach_local: int32 [524288], P(('gx', 'gy')), may hold values from 0 to 1023
- exch_coef: float32 [524288], P(('gx', 'gy')), may hold values from 0.2 to 1
- rate_left: float32 [32, 64], replicated, may hold values from -1 to 1
- rate_right: float32 [32, 64], replicated, may hold values from -1 to 1
- stoich: float32 [64, 32], replicated, may hold values from -0.75 to 0.75
Outputs:
- state_out: float32 [512, 256, 2048], P('gx', 'gy')
- stream_out: float32 [524288, 32], P(('gx', 'gy'))
Inputs may be any that keep to these rules, and one draw needn't show every extreme that they name: `reach_owner`: in the nodes of one device at most 64 have the same owner, and some owner gets exactly 64.
All inputs are finite; a program needn't handle non-finite values.
Results may differ from a plain program's by a relative error of at most 0.0003.
Values sent between devices are 32-bit elements; how exact they have to be, the bound alone decides.
A program may use at most 192 MiB of HBM per device.

v0:
```python
import functools

import jax
import jax.numpy as jnp
from jax import lax
from jax.experimental import pallas as pl
from jax.experimental.pallas import tpu as pltpu
from jax.sharding import PartitionSpec as P

MESH = pl.DeviceIdType.MESH
f32, bf16, i32 = jnp.float32, jnp.bfloat16, jnp.int32
VM = pl.BlockSpec(memory_space=pltpu.VMEM)
ANY = pl.BlockSpec(memory_space=pl.ANY)

CAP = 64
ROWS = 16
MSG = ROWS + 1


def iota(shape, dim):
    return lax.broadcasted_iota(i32, shape, dim)


def split(x):
    hi = x.astype(bf16)
    return hi, (x - hi.astype(f32)).astype(bf16)


def dot(a, b):
    return jnp.dot(a, b, preferred_element_type=f32)


def pack_kernel(owner, local, coef, stream_t, flat_out, msg, rows, buf, flat_v, flat_s, sem):
    groups = owner.shape[0]
    peers = msg.shape[0]
    sub, lane = iota((128, 128), 0), iota((128, 128), 1)
    upto = (sub <= lane).astype(bf16)
    ones = jnp.ones((128, 128), bf16)
    carry = jnp.zeros((128, 128), f32)
    for g in range(groups):
        mine = sub == owner[g : g + 1, :]
        onehot = mine.astype(f32).astype(bf16)
        count = dot(onehot, upto) + carry
        carry = carry + dot(onehot, ones)
        rank = jnp.sum(jnp.where(mine, count, 0.0), axis=0, keepdims=True)
        flat_v[g : g + 1, :] = owner[g : g + 1, :] * CAP + rank.astype(i32) - 1
    pltpu.make_async_copy(flat_v, flat_s, sem).start()
    flat_out[...] = flat_v[...]

    def fill(g, _):
        at = pl.multiple_of(g * 128, 128)
        block = jnp.concatenate(
            [
                stream_t[:, pl.ds(at, 128)],
                local[pl.ds(g, 1), :].astype(f32),
                coef[pl.ds(g, 1), :],
                jnp.zeros((94, 128), f32),
            ],
            axis=0,
        )
        rows[pl.ds(at, 128), :] = block.T
        return 0

    lax.fori_loop(0, groups, fill, 0)
    empty = jnp.where(lane == 32, -1.0, 0.0)

    def clear(g, _):
        buf[pl.ds(pl.multiple_of(g * 128, 128), 128), :] = empty
        return 0

    lax.fori_loop(0, buf.shape[0] // 128, clear, 0)
    pltpu.make_async_copy(flat_v, flat_s, sem).wait()

    def move(g, _):
        for j in range(128):
            buf[pl.ds(flat_s[g, j], 1), :] = rows[pl.ds(g * 128 + j, 1), :]
        return 0

    lax.fori_loop(0, groups, move, 0)
    lane16 = iota((16, 128), 1)
    mine16 = lane16 // 8 == (16 - iota((16, 128), 0)) % 16

    def form(t, _):
        at = pl.multiple_of(t * CAP, CAP)
        part = [buf[pl.ds(at + q * 16, 16), :] for q in range(4)]
        vals = part[3]
        vals = pltpu.roll(vals, 96, axis=1)
        for q in (2, 1):
            vals = jnp.where(lane16 < 32 * (q + 1), pltpu.roll(part[q], 32 * q, axis=1), vals)
        vals = jnp.where(lane16 < 32, part[0], vals)
        meta = jnp.zeros((16, 128), f32)
        for q in range(4):
            moved = pltpu.roll(part[q], (96 + 2 * q) % 128, axis=1)
            meta = jnp.where((lane16 >= 2 * q) & (lane16 < 2 * q + 2), moved, meta)
        for shift in (8, 16, 32, 64):
            meta = meta + pltpu.roll(meta, shift, axis=1)
        meta = jnp.where(mine16, meta, 0.0)
        msg[pl.ds(t, 1), pl.ds(0, ROWS), :] = vals[None]
        msg[pl.ds(t, 1), pl.ds(ROWS, 1), :] = jnp.sum(meta, axis=0, keepdims=True)[None]
        return 0

    lax.fori_loop(0, peers, form, 0, unroll=4)


def pack(owner, local, coef, stream_t, peers):
    groups = owner.shape[0]
    return pl.pallas_call(
        pack_kernel,
        out_shape=(
            jax.ShapeDtypeStruct((groups, 128), i32),
            jax.ShapeDtypeStruct((peers, MSG, 128), f32),
        ),
        in_specs=[VM] * 4,
        out_specs=(VM, VM),
        scratch_shapes=[
            pltpu.VMEM((groups * 128, 128), f32),
            pltpu.VMEM((peers * CAP, 128), f32),
            pltpu.VMEM((groups, 128), i32),
            pltpu.SMEM((groups, 128), i32),
            pltpu.SemaphoreType.DMA,
        ],
        compiler_params=pltpu.CompilerParams(vmem_limit_bytes=48 << 20),
        name="pack",
    )(owner, local, coef, stream_t)


GROUP = 4


def flux_of(messages, top, acc, put):
    columns = top.shape[0]
    lane16 = iota((16, 128), 1)
    vals, cols, coefs = [], [], []
    for m in messages:
        meta = jnp.broadcast_to(m[ROWS : ROWS + 1, :], (16, 128))
        meta = pltpu.roll(meta, 0, axis=1, stride=8, stride_axis=0)
        for q in range(4):
            vals.append(pltpu.roll(m[0:ROWS, :], (128 - 32 * q) % 128, axis=1) if q else m[0:ROWS, :])
            cols.append(jnp.broadcast_to(meta[:, 2 * q : 2 * q + 1], (16, 128)))
            coefs.append(jnp.broadcast_to(meta[:, 2 * q + 1 : 2 * q + 2], (16, 128)))
    vals = jnp.concatenate(vals, axis=0)
    cols = jnp.concatenate(cols, axis=0)
    coefs = jnp.concatenate(coefs, axis=0)
    slots = vals.shape[0]
    lane = iota((slots, 128), 1).astype(f32)
    onehot = jnp.concatenate(
        [jnp.where(cols == lane + 128.0 * b, 1.0, 0.0).astype(bf16) for b in range(columns // 128)], axis=1
    )
    picked = dot(onehot, top[...])
    picked = picked + pltpu.roll(picked, 96, axis=1)
    flux = jnp.where(lane < 32.0, coefs * (vals - picked), 0.0)
    low = flux - flux.astype(bf16).astype(f32)
    both = flux.astype(bf16).astype(f32) + pltpu.roll(low, 32, axis=1)
    both = both.T[0:64, :].astype(bf16)
    acc[...] += dot(both, onehot)
    for p in range(len(messages)):
        out = flux[64 * p : 64 * p + 16, :]
        for q in range(1, 4):
            out = out + pltpu.roll(flux[64 * p + 16 * q : 64 * p + 16 * q + 16, :], 32 * q, axis=1)
        put(p, out)


def top_of(state_top, top):
    high, low = split(state_top)
    lane = iota(state_top.shape, 1)
    high, low = high.astype(f32), pltpu.roll(low.astype(f32), 32, axis=1)
    top[...] = jnp.where(lane < 32, high, jnp.where(lane < 64, low, 0.0)).astype(bf16)


def exchange_kernel(
    msg, state_top, source, back, inbox, outbox, top, acc, send1, recv1, send2, recv2
):
    peers = msg.shape[0]
    size_y = lax.axis_size("gy")
    me = lax.axis_index("gx") * size_y + lax.axis_index("gy")

    def device(t):
        return (t // size_y, lax.rem(t, size_y))

    def send(d):
        to = lax.rem(me + d, peers)
        return pltpu.make_async_remote_copy(
            src_ref=msg.at[to],
            dst_ref=inbox.at[d],
            send_sem=send1,
            recv_sem=recv1.at[d],
            device_id=device(to),
            device_id_type=MESH,
        )

    def reply(d):
        to = lax.rem(me + peers - d, peers)
        return pltpu.make_async_remote_copy(
            src_ref=outbox.at[d],
            dst_ref=back.at[me],
            send_sem=send2,
            recv_sem=recv2,
            device_id=device(to),
            device_id_type=MESH,
        )

    def start(d, _):
        send(d).start()
        return 0

    lax.fori_loop(1, peers, start, 0)
    keep = pltpu.make_async_copy(msg.at[me], inbox.at[0], recv1.at[0])
    keep.start()
    columns = state_top.shape[0] * state_top.shape[1]
    top_of(state_top[...].reshape(columns, 128), top)
    acc[...] = jnp.zeros_like(acc)
    keep.wait()

    def work(c, first):
        for p in range(GROUP):
            if not (first and p == 0):
                send(c * GROUP + p).wait_recv()

        def put(p, value):
            outbox[pl.ds(c * GROUP + p, 1)] = value[None]

        flux_of([inbox[c * GROUP + p] for p in range(GROUP)], top, acc, put)
        for p in range(GROUP):
            if not (first and p == 0):
                reply(c * GROUP + p).start()

    work(0, True)

    def step(c, _):
        work(c, False)
        return 0

    lax.fori_loop(1, peers // GROUP, step, 0)
    own = pltpu.make_async_copy(outbox.at[0], back.at[me], recv1.at[0])
    own.start()
    source[...] = acc[0:32, :] + acc[32:64, :]
    own.wait()
    rest = pl.ds(0, peers - 1)
    pltpu.make_async_copy(msg.at[rest], msg.at[rest], send1).wait()
    pltpu.make_async_copy(outbox.at[rest], outbox.at[rest], send2).wait()
    pltpu.make_async_copy(back.at[rest], back.at[rest], recv2).wait()


def exchange(msg, state):
    peers = msg.shape[0]
    tile_x, tile_y, _ = state.shape
    columns = tile_x * tile_y
    return pl.pallas_call(
        exchange_kernel,
        grid=(1,),
        out_shape=(
            jax.ShapeDtypeStruct((32, columns), f32),
            jax.ShapeDtypeStruct((peers, ROWS, 128), f32),
        ),
        in_specs=[VM, pl.BlockSpec((tile_x, tile_y, 128), lambda i: (0, 0, 0))],
        out_specs=(VM, VM),
        scratch_shapes=[
            pltpu.VMEM((peers, MSG, 128), f32),
            pltpu.VMEM((peers, ROWS, 128), f32),
            pltpu.VMEM((columns, 128), bf16),
            pltpu.VMEM((64, columns), f32),
            pltpu.SemaphoreType.DMA,
            pltpu.SemaphoreType.DMA((peers,)),
            pltpu.SemaphoreType.DMA,
            pltpu.SemaphoreType.DMA,
        ],
        compiler_params=pltpu.CompilerParams(has_side_effects=True, vmem_limit_bytes=48 << 20),
        name="exchange",
    )(msg, state)


def unpack_kernel(flat, back, stream_t, out, buf, rows):
    groups = flat.shape[0]
    peers = back.shape[0]

    def spread(t, _):
        m = back[t]
        at = pl.multiple_of(t * CAP, CAP)
        for q in range(4):
            buf[pl.ds(at + 16 * q, 16), :] = pltpu.roll(m, 128 - 32 * q, axis=1) if q else m
        return 0

    lax.fori_loop(0, peers, spread, 0, unroll=4)

    def move(g, _):
        at = pl.multiple_of(g * 128, 128)
        for j in range(128):
            rows[pl.ds(j, 1), :] = buf[pl.ds(flat[g, j], 1), :]
        out[:, pl.ds(at, 128)] = stream_t[:, pl.ds(at, 128)] - 0.5 * rows[...].T[0:32, :]
        return 0

    lax.fori_loop(0, groups, move, 0)


def unpack(flat, back, stream_t):
    peers = back.shape[0]
    return pl.pallas_call(
        unpack_kernel,
        out_shape=jax.ShapeDtypeStruct(stream_t.shape, f32),
        in_specs=[pl.BlockSpec(memory_space=pltpu.SMEM), VM, VM],
        out_specs=VM,
        scratch_shapes=[pltpu.VMEM((peers * CAP, 128), f32), pltpu.VMEM((128, 128), f32)],
        compiler_params=pltpu.CompilerParams(vmem_limit_bytes=48 << 20),
        name="unpack",
    )(flat, back, stream_t)


XB = 8


def columns_kernel(
    st, up, dn, x_low, x_high, y_low, y_high, lat, count, diff, scale, source, left, right, stoich_t,
    out, w_first, w_low, s_high, s_low, lat_col, count_col, scale_col, rhs, coef, iface,
):
    i = pl.program_id(0)
    last = pl.num_programs(0) - 1
    sub, lane = iota((128, 128), 0), iota((128, 128), 1)

    @pl.when(i == 0)
    def _():
        inside = iota((128, 256), 0) // 32 == iota((128, 256), 1) // 64

        def spread(w):
            wide = jnp.concatenate([w] * 4, axis=1)
            return jnp.where(inside, jnp.concatenate([wide] * 4, axis=0), 0.0)

        high, low = split(jnp.concatenate([spread(left[...]), spread(right[...])], axis=1))
        w_first[0:128, :] = high
        w_first[128:256, :] = high
        w_low[...] = low
        high, low = split(spread(stoich_t[...]).T)
        s_high[...] = high
        s_low[...] = low

        def turned(a):
            a = jnp.concatenate([a, jnp.zeros((32, 96), f32)], axis=1)
            return jnp.concatenate([a, jnp.zeros((96, 128), f32)], axis=0).T

        lat_t, count_t = turned(lat[...]), turned(count[...].astype(f32))
        for g in range(4):
            lat_col[g] = pltpu.roll(lat_t, (128 - XB * g) % 128, axis=1)[0:32, :]
            count_col[g] = pltpu.roll(count_t, (128 - XB * g) % 128, axis=1)[0:32, :]
        scale_col[...] = jnp.broadcast_to(
            jnp.sum(
                jnp.where(iota((32, 32), 0) == iota((32, 32), 1), jnp.broadcast_to(scale[...], (32, 32)), 0.0),
                axis=1,
                keepdims=True,
            ),
            (32, 128),
        )

    row = iota((32, 128), 0)
    lats = [jnp.broadcast_to(lat_col[i, :, x : x + 1], (32, 128)) for x in range(XB)]
    for cb in range(2):
        for j in range(16):
            at = slice(128 * j, 128 * j + 128)
            parts = []
            for x in range(4 * cb, 4 * cb + 4):
                s = st[x, :, at]
                before = st[x - 1, :, at] if x else jnp.where(i == 0, x_low[0, :, at], up[0, :, at])
                after = st[x + 1, :, at] if x < XB - 1 else jnp.where(i == last, x_high[0, :, at], dn[0, :, at])
                lower = jnp.where(row == 0, y_low[x, :, at], pltpu.roll(s, 1, axis=0))
                upper = jnp.where(row == 31, y_high[x, :, at], pltpu.roll(s, 31, axis=0))
                parts.append(s + lats[x] * ((before + after) + (lower + upper) - 4.0 * s))
            rhs[at, 128 * cb : 128 * cb + 128] = jnp.concatenate(parts, axis=0).T
        counts = jnp.concatenate([count[pl.ds(XB * i + 4 * cb + x, 1), :] for x in range(4)], axis=1)
        d = diff[4 * cb : 4 * cb + 4].reshape(128, 64)
        d = jnp.concatenate([d, jnp.zeros((128, 64), f32)], axis=1).T[0:64, :]
        iface[:, 128 * cb : 128 * cb + 128] = jnp.where(iota((64, 128), 0) + 1 < counts, d, 0.0)
    rhs[0:32, :] += source[...]

    scales = jnp.concatenate([scale_col[...]] * 2, axis=1)
    zero = jnp.zeros((32, 256), f32)

    def upper_at(k):
        return scales * iface[k : k + 1, :]

    def cell(k):
        return slice(32 * k, 32 * k + 32)

    c, d, u_before = zero, zero, zero
    e_c, e_d, u_here = zero, zero, upper_at(63)
    for k in range(32):
        u = upper_at(k)
        r = 1.0 / (1.0 + u + u_before * (1.0 - c))
        d = (rhs[cell(k), :] + u_before * d) * r
        c = u * r
        u_before = u
        m = 63 - k
        v = upper_at(m - 1)
        r = 1.0 / (1.0 + v + u_here * (1.0 - e_c))
        e_d = (rhs[cell(m), :] + u_here * e_d) * r
        e_c = v * r
        u_here = v
        if k < 31:
            coef[cell(k), :] = c
            rhs[cell(k), :] = d
            coef[cell(m), :] = e_c
            rhs[cell(m), :] = e_d
    low = (d + c * e_d) / (1.0 - c * e_c)
    high = e_d + e_c * low
    rhs[cell(31), :] = low
    rhs[cell(32), :] = high
    for k in range(30, -1, -1):
        low = rhs[cell(k), :] + coef[cell(k), :] * low
        rhs[cell(k), :] = low
        m = 63 - k
        high = rhs[cell(m), :] + coef[cell(m), :] * high
        rhs[cell(m), :] = high

    for cb in range(2):
        counts = jnp.concatenate(
            [jnp.broadcast_to(count_col[i, :, x : x + 1], (32, 128)) for x in range(4 * cb, 4 * cb + 4)], axis=0
        )
        depth = counts - (lane // 32).astype(f32)
        for j in range(16):
            at = slice(128 * j, 128 * j + 128)
            x = rhs[at, 128 * cb : 128 * cb + 128].T
            high, low = split(x)
            both = dot(jnp.concatenate([high, low], axis=1), w_first[...]) + dot(high, w_low[...])
            high, low = split(both[:, 0:256] * both[:, 256:512])
            change = dot(high, s_high[...]) + dot(low, s_high[...]) + dot(high, s_low[...])
            new = x + jnp.where(depth > 4.0 * j, 0.1, 0.0) * change
            for p in range(4):
                out[4 * cb + p, :, at] = new[32 * p : 32 * p + 32, :]


def columns(state, x_low, x_high, y_low, y_high, lat, count, diffusion, scale, source, left, right, stoich_t):
    tile_x, tile_y, width = state.shape
    steps = tile_x // XB
    whole = lambda shape: pl.BlockSpec(shape, lambda i: (0,) * len(shape))
    return pl.pallas_call(
        columns_kernel,
        grid=(steps,),
        out_shape=jax.ShapeDtypeStruct(state.shape, f32),
        in_specs=[
            pl.BlockSpec((XB, tile_y, width), lambda i: (i, 0, 0)),
            pl.BlockSpec((1, tile_y, width), lambda i: (jnp.maximum(XB * i - 1, 0), 0, 0)),
            pl.BlockSpec((1, tile_y, width), lambda i: (jnp.minimum(XB * i + XB, tile_x - 1), 0, 0)),
            whole(x_low.shape),
            whole(x_high.shape),
            pl.BlockSpec((XB, 1, width), lambda i: (i, 0, 0)),
            pl.BlockSpec((XB, 1, width), lambda i: (i, 0, 0)),
            whole(lat.shape),
            whole(count.shape),
            pl.BlockSpec((XB, tile_y, diffusion.shape[2]), lambda i: (i, 0, 0)),
            whole(scale.shape),
            pl.BlockSpec((32, XB * tile_y), lambda i: (0, i)),
            whole(left.shape),
            whole(right.shape),
            whole(stoich_t.shape),
        ],
        out_specs=pl.BlockSpec((XB, tile_y, width), lambda i: (i, 0, 0)),
        scratch_shapes=[
            pltpu.VMEM((256, 512), bf16),
            pltpu.VMEM((128, 512), bf16),
            pltpu.VMEM((256, 128), bf16),
            pltpu.VMEM((256, 128), bf16),
            pltpu.VMEM((steps, 32, 128), f32),
            pltpu.VMEM((steps, 32, 128), f32),
            pltpu.VMEM((32, 128), f32),
            pltpu.VMEM((width, XB * tile_y), f32),
            pltpu.VMEM((width, XB * tile_y), f32),
            pltpu.VMEM((64, XB * tile_y), f32),
        ],
        compiler_params=pltpu.CompilerParams(vmem_limit_bytes=56 << 20),
        name="columns",
    )(state, state, state, x_low, x_high, y_low, y_high, lat, count, diffusion, scale, source, left, right, stoich_t)


def halo(state):
    out = []
    for axis, dim in (("gx", 0), ("gy", 1)):
        count = lax.axis_size(axis)
        forward = [(i, i + 1) for i in range(count - 1)]
        backward = [(target, source) for source, target in forward]
        end = state.shape[dim] - 1
        out.append(lax.ppermute(lax.slice_in_dim(state, end, end + 1, axis=dim), axis, forward))
        out.append(lax.ppermute(lax.slice_in_dim(state, 0, 1, axis=dim), axis, backward))
    return out


def body(
    state,
    lat_coef,
    diffusion,
    layer_count,
    species_scale,
    stream,
    reach_owner,
    reach_local,
    exch_coef,
    rate_left,
    rate_right,
    stoich,
):
    peers = lax.axis_size("gx") * lax.axis_size("gy")
    x_low, x_high, y_low, y_high = halo(state)
    stream_t = stream.T
    flat, msg = pack(
        reach_owner.reshape(-1, 128), reach_local.reshape(-1, 128), exch_coef.reshape(-1, 128), stream_t, peers
    )
    source, back = exchange(msg, state)
    state_out = columns(
        state, x_low, x_high, y_low, y_high, lat_coef, layer_count, diffusion, species_scale[None, :], source,
        rate_left, rate_right, stoich.T,
    )
    stream_out = unpack(flat, back, stream_t).T
    return (state_out, stream_out)


def solution(mesh):
    return jax.shard_map(
        body,
        mesh=mesh,
        in_specs=(
            P("gx", "gy", None),
            P("gx", "gy"),
            P("gx", "gy", None),
            P("gx", "gy"),
            P(),
            P(("gx", "gy"), None),
            P(("gx", "gy"), None),
            P(("gx", "gy")),
            P(("gx", "gy")),
            P(),
            P(),
            P(),
        ),
        out_specs=(P("gx", "gy", None), P(("gx", "gy"), None)),
        check_vma=False,
    )
```

profile of v0, /device:TPU:1, one launch (start us, length us, event | category | flops | bytes accessed | tf_op | source)
XLA Modules:
  0.0 157.2 jit_solution(17995286477688554191)
XLA Ops:
  0.6 0.0 copy-start.1
  0.6 1.1 fusion.1
  1.8 1.3 collective-permute-start.1
  3.1 4.7 %collective-permute-start = (f32[1,32,2048]{2,1,0:T(8,128)S(1)}, f32[1,32,2048]{2,1,0:T(8,128)S(1)}, u32[]{:S(2)}, u32[]{:S(2)}) collective-permute-start(f32[1,32,2048]{2,1,0:T(8,128)S(1)} %get-tuple-element.13), channel_id=1, source_target_pairs={{0,8},{8,16},{16,24},{24,32},{32,40},{40,48},{48,56},{56,64},{64,7... | collective-permute-start | bytes 786440 | tf_op jit(solution)/shard_map/ppermute | solution.py:478
  7.8 2.7 %fusion = (f32[32,1,2048]{2,1,0:T(1,128)S(1)}, f32[32,1,2048]{2,1,0:T(1,128)S(1)}) fusion(f32[32,32,2048]{2,1,0:T(8,128)} %dn.1), kind=kLoop, calls=%fused_computation | loop fusion | bytes 1048576 | tf_op jit(solution)/shard_map/slice | solution.py:479
  10.4 3.2 %collective-permute-start.3 = (f32[32,1,2048]{2,1,0:T(1,128)S(1)}, f32[32,1,2048]{2,1,0:T(1,128)S(1)}, u32[]{:S(2)}, u32[]{:S(2)}) collective-permute-start(f32[32,1,2048]{2,1,0:T(1,128)S(1)} %get-tuple-element.10), channel_id=1, source_target_pairs={{1,0},{2,1},{3,2},{4,3},{5,4},{6,5},{7,6},{9,8},{10,9},{11,10},{12... | collective-permute-start | bytes 786440 | tf_op jit(solution)/shard_map/ppermute | solution.py:479
  13.7 3.5 %collective-permute-start.2 = (f32[32,1,2048]{2,1,0:T(1,128)S(1)}, f32[32,1,2048]{2,1,0:T(1,128)S(1)}, u32[]{:S(2)}, u32[]{:S(2)}) collective-permute-start(f32[32,1,2048]{2,1,0:T(1,128)S(1)} %get-tuple-element.11), channel_id=1, source_target_pairs={{0,1},{1,2},{2,3},{3,4},{4,5},{5,6},{6,7},{8,9},{9,10},{10,11},{11... | collective-permute-start | bytes 786440 | tf_op jit(solution)/shard_map/ppermute | solution.py:478
  17.2 0.0 copy-start
  17.2 1.0 copy-done
  18.2 0.0 copy-start.3
  18.2 0.7 copy-done.3
  19.0 0.0 copy-start.4
  19.0 0.7 copy-done.4
  19.7 0.7 copy-done.5
  20.4 20.1 %pack.1 = (s32[32,128]{1,0:T(8,128)S(1)}, f32[128,17,128]{2,1,0:T(8,128)S(1)}) custom-call(s32[32,128]{1,0:T(8,128)S(1)} %bitcast.9, s32[32,128]{1,0:T(8,128)S(1)} %bitcast.10, f32[32,128]{1,0:T(8,128)S(1)} %bitcast.11, f32[32,4096]{1,0:T(8,128)S(1)} %bitcast.7), custom_call_target="tpu_custom_call" | custom-call | tf_op jit(solution)/shard_map/pack/pallas_call | solution.py:107
  40.5 63.9 %exchange.1 = (f32[32,1024]{1,0:T(8,128)S(1)}, f32[128,16,128]{2,1,0:T(8,128)S(1)}) custom-call(f32[128,17,128]{2,1,0:T(8,128)S(1)} %get-tuple-element.6.msg, f32[32,32,2048]{2,1,0:T(8,128)} %dn.1), custom_call_target="tpu_custom_call" | custom-call | tf_op jit(solution)/shard_map/exchange/pallas_call | solution.py:248
  104.4 0.0 copy-start.2
  104.4 0.0 copy-done.1
  104.4 10.1 %unpack.1 = f32[32,4096]{1,0:T(8,128)} custom-call(s32[32,128]{1,0:T(8,128)S(1)} %get-tuple-element.8.flat, f32[128,16,128]{2,1,0:T(8,128)S(1)} %get-tuple-element.9.back, f32[32,4096]{1,0:T(8,128)S(1)} %bitcast.8), custom_call_target="tpu_custom_call" | custom-call | tf_op jit(solution)/shard_map/unpack/pallas_call | solution.py:297
  114.5 0.0 copy-done.2
  114.5 0.0 collective-permute-done.1.x_high
  114.5 0.0 collective-permute-done.x_low
  114.6 0.0 copy-start.7
  114.6 0.0 collective-permute-done.3.y_high
  114.6 0.0 copy-start.8
  114.6 0.0 collective-permute-done.2.y_low
  114.6 0.0 copy-start.9
  114.6 0.6 copy-done.6
  115.2 0.1 copy-done.7
  115.3 0.1 copy-done.8
  115.4 0.1 copy-done.9
  115.5 41.6 %columns.1 = f32[32,32,2048]{2,1,0:T(8,128)} custom-call(f32[32,32,2048]{2,1,0:T(8,128)} %dn.1, f32[32,32,2048]{2,1,0:T(8,128)} %dn.1, f32[32,32,2048]{2,1,0:T(8,128)} %dn.1, f32[1,32,2048]{2,1,0:T(8,128)} %copy-done.7, f32[1,32,2048]{2,1,0:T(8,128)} %copy-done.6, f32[32,1,2048]{2,1,0:T(1,128)} %copy-done.9, f32[32,1,2048]{2,1,0:T(1,128)} %copy-done.8, ...), custom_call_target="tpu_custom_call" | custom-call | tf_op jit(solution)/shard_map/columns/pallas_call | solution.py:432
  (2 shorter events, 0.0 us)
Async XLA Ops:
  0.6 103.8 %copy-start.1 = (f32[4096,32]{0,1:T(8,128)S(1)}, f32[4096,32]{0,1:T(8,128)}, u32[]{:S(2)}) copy-start(f32[4096,32]{0,1:T(8,128)} %param.17) | copy-start | bytes 1572868
  1.8 112.8 %collective-permute-start.1 = (f32[1,32,2048]{2,1,0:T(8,128)S(1)}, f32[1,32,2048]{2,1,0:T(8,128)S(1)}, u32[]{:S(2)}, u32[]{:S(2)}) collective-permute-start(f32[1,32,2048]{2,1,0:T(8,128)S(1)} %get-tuple-element.12), channel_id=1, source_target_pairs={{8,0},{16,8},{24,16},{32,24},{40,32},{48,40},{56,48},{64,56},{72,6... | collective-permute-start | bytes 786440 | tf_op jit(solution)/shard_map/ppermute | solution.py:479
  3.1 111.5 %collective-permute-start = (f32[1,32,2048]{2,1,0:T(8,128)S(1)}, f32[1,32,2048]{2,1,0:T(8,128)S(1)}, u32[]{:S(2)}, u32[]{:S(2)}) collective-permute-start(f32[1,32,2048]{2,1,0:T(8,128)S(1)} %get-tuple-element.13), channel_id=1, source_target_pairs={{0,8},{8,16},{16,24},{24,32},{32,40},{40,48},{48,56},{56,64},{64,7... | collective-permute-start | bytes 786440 | tf_op jit(solution)/shard_map/ppermute | solution.py:478
  10.4 104.1 %collective-permute-start.3 = (f32[32,1,2048]{2,1,0:T(1,128)S(1)}, f32[32,1,2048]{2,1,0:T(1,128)S(1)}, u32[]{:S(2)}, u32[]{:S(2)}) collective-permute-start(f32[32,1,2048]{2,1,0:T(1,128)S(1)} %get-tuple-element.10), channel_id=1, source_target_pairs={{1,0},{2,1},{3,2},{4,3},{5,4},{6,5},{7,6},{9,8},{10,9},{11,10},{12... | collective-permute-start | bytes 786440 | tf_op jit(solution)/shard_map/ppermute | solution.py:479
  13.7 100.9 %collective-permute-start.2 = (f32[32,1,2048]{2,1,0:T(1,128)S(1)}, f32[32,1,2048]{2,1,0:T(1,128)S(1)}, u32[]{:S(2)}, u32[]{:S(2)}) collective-permute-start(f32[32,1,2048]{2,1,0:T(1,128)S(1)} %get-tuple-element.11), channel_id=1, source_target_pairs={{0,1},{1,2},{2,3},{3,4},{4,5},{5,6},{6,7},{8,9},{9,10},{10,11},{11... | collective-permute-start | bytes 786440 | tf_op jit(solution)/shard_map/ppermute | solution.py:478
  17.2 1.0 copy-start
  18.2 0.7 copy-start.3
  19.0 0.7 copy-start.4
  19.7 0.7 copy-start.5
  104.4 10.1 %copy-start.2 = (f32[32,1024]{1,0:T(8,128)}, f32[32,1024]{1,0:T(8,128)S(1)}, u32[]{:S(2)}) copy-start(f32[32,1024]{1,0:T(8,128)S(1)} %get-tuple-element.7.source) | copy-start | bytes 393220
  114.5 0.7 copy-start.6
  114.6 0.8 copy-start.7
  114.6 0.9 copy-start.8
  114.6 0.9 copy-start.9
where the time goes:
time: 158 us; the launch traced here: 157 us
  Pallas kernels  136 us (86%)
  starting transfers between devices  12.7 us (8%)
  local copies, waits for them, and re-layouts  7.91 us (5%)
    pallas_call x1, Pallas kernels, exchange(): pl.pallas_call(exchange_kernel, grid=(1,), out_shape=(jax.ShapeDtypeStruc...  63.9 us
    pallas_call x1, Pallas kernels, columns(): pl.pallas_call(columns_kernel, grid=(steps,), out_shape=jax.ShapeDtypeStr...  41.6 us
    pallas_call x1, Pallas kernels, pack(): pl.pallas_call(pack_kernel, out_shape=(jax.ShapeDtypeStruct((groups, 128)...  20.1 us
    pallas_call x1, Pallas kernels, unpack(): pl.pallas_call(unpack_kernel, out_shape=jax.ShapeDtypeStruct(stream_t.sha...  10.1 us
    ppermute x2, starting transfers between devices, halo(): lax.ppermute(lax.slice_in_dim(state, end, end + 1, axis=dim), axis, forward)  8.2 us
    ppermute x2, starting transfers between devices, halo(): lax.ppermute(lax.slice_in_dim(state, 0, 1, axis=dim), axis, backward)  4.51 us
    unnamed x20, local copies, waits for them, and re-layouts  4.12 us
    slice x2, local copies, waits for them, and re-layouts, halo(): lax.slice_in_dim(state, 0, 1, axis=dim)  3.8 us
  transfers between devices with their start and end apart: 4, of which 0 were waited for; matrix products, arithmetic and copies ran while one was open for 2% of the time, Pallas kernels for 60%

commit v1 on v0

--- a/solution.py
+++ b/solution.py
@@ -15,6 +15,8 @@
 CAP = 64
 ROWS = 16
 MSG = ROWS + 1
+FORM = 16
+BATCH = 8
 
 
 def iota(shape, dim):
@@ -77,29 +79,30 @@
         return 0
 
     lax.fori_loop(0, groups, move, 0)
-    lane16 = iota((16, 128), 1)
-    mine16 = lane16 // 8 == (16 - iota((16, 128), 0)) % 16
+    lanes = iota((FORM * 16, 128), 1)
+    spot = lanes // 8 == (16 - iota((FORM * 16, 128), 0) % 16) % 16
 
     def form(t, _):
-        at = pl.multiple_of(t * CAP, CAP)
-        part = [buf[pl.ds(at + q * 16, 16), :] for q in range(4)]
-        vals = part[3]
-        vals = pltpu.roll(vals, 96, axis=1)
+        at = pl.multiple_of(t * FORM * CAP, FORM * CAP)
+        part = buf[pl.ds(at, FORM * CAP), :].reshape(FORM, 4, 16, 128)
+        part = [part[:, q].reshape(FORM * 16, 128) for q in range(4)]
+        vals = pltpu.roll(part[3], 96, axis=1)
         for q in (2, 1):
-            vals = jnp.where(lane16 < 32 * (q + 1), pltpu.roll(part[q], 32 * q, axis=1), vals)
-        vals = jnp.where(lane16 < 32, part[0], vals)
-        meta = jnp.zeros((16, 128), f32)
+            vals = jnp.where(lanes < 32 * (q + 1), pltpu.roll(part[q], 32 * q, axis=1), vals)
+        vals = jnp.where(lanes < 32, part[0], vals)
+        meta = jnp.zeros((FORM * 16, 128), f32)
         for q in range(4):
             moved = pltpu.roll(part[q], (96 + 2 * q) % 128, axis=1)
-            meta = jnp.where((lane16 >= 2 * q) & (lane16 < 2 * q + 2), moved, meta)
+            meta = jnp.where((lanes >= 2 * q) & (lanes < 2 * q + 2), moved, meta)
         for shift in (8, 16, 32, 64):
             meta = meta + pltpu.roll(meta, shift, axis=1)
-        meta = jnp.where(mine16, meta, 0.0)
-        msg[pl.ds(t, 1), pl.ds(0, ROWS), :] = vals[None]
-        msg[pl.ds(t, 1), pl.ds(ROWS, 1), :] = jnp.sum(meta, axis=0, keepdims=True)[None]
-        return 0
-
-    lax.fori_loop(0, peers, form, 0, unroll=4)
+        meta = jnp.sum(jnp.where(spot, meta, 0.0).reshape(FORM, 16, 128), axis=1)
+        to = pl.ds(pl.multiple_of(t * FORM, FORM), FORM)
+        msg[to, pl.ds(0, ROWS), :] = vals.reshape(FORM, 16, 128)
+        msg[to, pl.ds(ROWS, 1), :] = meta[:, None, :]
+        return 0
+
+    lax.fori_loop(0, peers // FORM, form, 0)
 
 
 def pack(owner, local, coef, stream_t, peers):
@@ -124,53 +127,82 @@
     )(owner, local, coef, stream_t)
 
 
-GROUP = 4
-
-
 def flux_of(messages, top, acc, put):
-    columns = top.shape[0]
-    lane16 = iota((16, 128), 1)
-    vals, cols, coefs = [], [], []
-    for m in messages:
-        meta = jnp.broadcast_to(m[ROWS : ROWS + 1, :], (16, 128))
-        meta = pltpu.roll(meta, 0, axis=1, stride=8, stride_axis=0)
-        for q in range(4):
-            vals.append(pltpu.roll(m[0:ROWS, :], (128 - 32 * q) % 128, axis=1) if q else m[0:ROWS, :])
-            cols.append(jnp.broadcast_to(meta[:, 2 * q : 2 * q + 1], (16, 128)))
-            coefs.append(jnp.broadcast_to(meta[:, 2 * q + 1 : 2 * q + 2], (16, 128)))
-    vals = jnp.concatenate(vals, axis=0)
-    cols = jnp.concatenate(cols, axis=0)
-    coefs = jnp.concatenate(coefs, axis=0)
-    slots = vals.shape[0]
-    lane = iota((slots, 128), 1).astype(f32)
-    onehot = jnp.concatenate(
-        [jnp.where(cols == lane + 128.0 * b, 1.0, 0.0).astype(bf16) for b in range(columns // 128)], axis=1
+    count = len(messages)
+    rows = count * ROWS
+    lane = iota((rows, 128), 1)
+    lane_f, place, side = lane.astype(f32), lane // 32, (lane // 64).astype(f32)
+    vals = jnp.concatenate([m[0:ROWS, :] for m in messages], axis=0)
+    meta = jnp.concatenate(
+        [
+            pltpu.roll(jnp.broadcast_to(m[ROWS : ROWS + 1, :], (ROWS, 128)), 0, axis=1, stride=8, stride_axis=0)
+            for m in messages
+        ],
+        axis=0,
     )
+
+    def by_place(parts):
+        out = parts[3]
+        for q in (2, 1, 0):
+            out = jnp.where(place == q, parts[q], out)
+        return out
+
+    onehots, parts, coefs = [], [], []
+    for q in range(4):
+        column = jnp.broadcast_to(meta[:, 2 * q : 2 * q + 1], (rows, 128))
+        part = jnp.floor(column * (1.0 / 256.0))
+        low = column - 256.0 * part
+        onehots.append(
+            jnp.concatenate(
+                [jnp.where(low == lane_f + 128.0 * b, 1.0, 0.0).astype(bf16) for b in range(2)], axis=1
+            )
+        )
+        parts.append(part)
+        coefs.append(jnp.broadcast_to(meta[:, 2 * q + 1 : 2 * q + 2], (rows, 128)))
+    onehot = jnp.concatenate(onehots, axis=0)
     picked = dot(onehot, top[...])
-    picked = picked + pltpu.roll(picked, 96, axis=1)
-    flux = jnp.where(lane < 32.0, coefs * (vals - picked), 0.0)
-    low = flux - flux.astype(bf16).astype(f32)
-    both = flux.astype(bf16).astype(f32) + pltpu.roll(low, 32, axis=1)
-    both = both.T[0:64, :].astype(bf16)
-    acc[...] += dot(both, onehot)
-    for p in range(len(messages)):
-        out = flux[64 * p : 64 * p + 16, :]
-        for q in range(1, 4):
-            out = out + pltpu.roll(flux[64 * p + 16 * q : 64 * p + 16 * q + 16, :], 32 * q, axis=1)
-        put(p, out)
+    tops = []
+    for q in range(4):
+        p = picked[rows * q : rows * q + rows, :]
+        p = jnp.where(parts[q] == side, p[:, 0:128], 0.0) + jnp.where(parts[q] == side + 2.0, p[:, 128:256], 0.0)
+        p = p + pltpu.roll(p, 64, axis=1)
+        tops.append(p + pltpu.roll(p, 32, axis=1))
+    flux = by_place(coefs) * (vals - by_place(tops))
+    for p in range(count):
+        put(p, flux[ROWS * p : ROWS * p + ROWS, :])
+    flux_t, part_t = flux.T, by_place(parts).T
+    flux_t = jnp.concatenate([flux_t[32 * q : 32 * q + 32, :] for q in range(4)], axis=1)
+    part_t = jnp.concatenate([part_t[32 * q : 32 * q + 1, :] for q in range(4)], axis=1)
+    high = flux_t.astype(bf16).astype(f32)
+    both = jnp.concatenate([high, flux_t - high], axis=0)
+    spread = jnp.concatenate([jnp.where(part_t == float(g), both, 0.0).astype(bf16) for g in range(4)], axis=0)
+    acc[...] += dot(spread, onehot)
 
 
 def top_of(state_top, top):
-    high, low = split(state_top)
-    lane = iota(state_top.shape, 1)
-    high, low = high.astype(f32), pltpu.roll(low.astype(f32), 32, axis=1)
-    top[...] = jnp.where(lane < 32, high, jnp.where(lane < 64, low, 0.0)).astype(bf16)
+    lane = iota((256, 128), 1)
+    quarters = []
+    for g in range(4):
+        t = jnp.where(lane < 32, state_top[256 * g : 256 * g + 256, :], 0.0)
+        high = t.astype(bf16).astype(f32)
+        quarters.append(high + pltpu.roll(t - high, 32, axis=1))
+    top[...] = jnp.concatenate(
+        [quarters[g] + pltpu.roll(quarters[g + 1], 64, axis=1) for g in (0, 2)], axis=1
+    ).astype(bf16)
+
+
+def source_of(acc, source):
+    for g in range(4):
+        source[:, 256 * g : 256 * g + 256] = acc[64 * g : 64 * g + 32, :] + acc[64 * g + 32 : 64 * g + 64, :]
 
 
 def exchange_kernel(
-    msg, state_top, source, back, inbox, outbox, top, acc, send1, recv1, send2, recv2
+    msg, state_top, state, none_x, none_y, source, back, x_low, x_high, y_low, y_high,
+    inbox, outbox, top, acc, send1, recv1, send2, recv2, send_edge, recv_edge,
 ):
     peers = msg.shape[0]
+    size_x = lax.axis_size("gx")
+    ends = state.shape[0] - 1, state.shape[1] - 1
     size_y = lax.axis_size("gy")
     me = lax.axis_index("gx") * size_y + lax.axis_index("gy")
 
@@ -199,11 +231,36 @@
             device_id_type=MESH,
         )
 
+    gx, gy = lax.axis_index("gx"), lax.axis_index("gy")
+    edges = [
+        (state.at[pl.ds(ends[0], 1)], x_low, (lax.rem(gx + 1, size_x), gy), gx < size_x - 1, gx > 0),
+        (state.at[pl.ds(0, 1)], x_high, (lax.rem(gx + size_x - 1, size_x), gy), gx > 0, gx < size_x - 1),
+        (state.at[:, pl.ds(ends[1], 1)], y_low, (gx, lax.rem(gy + 1, size_y)), gy < size_y - 1, gy > 0),
+        (state.at[:, pl.ds(0, 1)], y_high, (gx, lax.rem(gy + size_y - 1, size_y)), gy > 0, gy < size_y - 1),
+    ]
+
+    def edge(n):
+        block, to, device_id, _, _ = edges[n]
+        return pltpu.make_async_remote_copy(
+            src_ref=block,
+            dst_ref=to,
+            send_sem=send_edge.at[n],
+            recv_sem=recv_edge.at[n],
+            device_id=device_id,
+            device_id_type=MESH,
+        )
+
+    def outside(n):
+        return pltpu.make_async_copy(none_x if n < 2 else none_y, edges[n][1], recv_edge.at[n])
+
     def start(d, _):
         send(d).start()
         return 0
 
     lax.fori_loop(1, peers, start, 0)
+    for n in range(4):
+        pl.when(edges[n][3])(edge(n).start)
+        pl.when(jnp.logical_not(edges[n][4]))(outside(n).start)
     keep = pltpu.make_async_copy(msg.at[me], inbox.at[0], recv1.at[0])
     keep.start()
     columns = state_top.shape[0] * state_top.shape[1]
@@ -212,17 +269,17 @@
     keep.wait()
 
     def work(c, first):
-        for p in range(GROUP):
+        for p in range(BATCH):
             if not (first and p == 0):
-                send(c * GROUP + p).wait_recv()
+                send(c * BATCH + p).wait_recv()
 
         def put(p, value):
-            outbox[pl.ds(c * GROUP + p, 1)] = value[None]
-
-        flux_of([inbox[c * GROUP + p] for p in range(GROUP)], top, acc, put)
-        for p in range(GROUP):
+            outbox[pl.ds(c * BATCH + p, 1)] = value[None]
+
+        flux_of([inbox[c * BATCH + p] for p in range(BATCH)], top, acc, put)
+        for p in range(BATCH):
             if not (first and p == 0):
-                reply(c * GROUP + p).start()
+                reply(c * BATCH + p).start()
 
     work(0, True)
 
@@ -230,11 +287,15 @@
         work(c, False)
         return 0
 
-    lax.fori_loop(1, peers // GROUP, step, 0)
+    lax.fori_loop(1, peers // BATCH, step, 0)
     own = pltpu.make_async_copy(outbox.at[0], back.at[me], recv1.at[0])
     own.start()
-    source[...] = acc[0:32, :] + acc[32:64, :]
+    source_of(acc, source)
     own.wait()
+    for n in range(4):
+        pl.when(edges[n][3])(edge(n).wait_send)
+        pl.when(edges[n][4])(edge(n).wait_recv)
+        pl.when(jnp.logical_not(edges[n][4]))(outside(n).wait)
     rest = pl.ds(0, peers - 1)
     pltpu.make_async_copy(msg.at[rest], msg.at[rest], send1).wait()
     pltpu.make_async_copy(outbox.at[rest], outbox.at[rest], send2).wait()
@@ -243,30 +304,37 @@
 
 def exchange(msg, state):
     peers = msg.shape[0]
-    tile_x, tile_y, _ = state.shape
-    columns = tile_x * tile_y
+    tile_x, tile_y, width = state.shape
+    edge_x = jax.ShapeDtypeStruct((1, tile_y, width), f32)
+    edge_y = jax.ShapeDtypeStruct((tile_x, 1, width), f32)
     return pl.pallas_call(
         exchange_kernel,
         grid=(1,),
         out_shape=(
-            jax.ShapeDtypeStruct((32, columns), f32),
+            jax.ShapeDtypeStruct((32, tile_x * tile_y), f32),
             jax.ShapeDtypeStruct((peers, ROWS, 128), f32),
+            edge_x,
+            edge_x,
+            edge_y,
+            edge_y,
         ),
-        in_specs=[VM, pl.BlockSpec((tile_x, tile_y, 128), lambda i: (0, 0, 0))],
-        out_specs=(VM, VM),
+        in_specs=[VM, pl.BlockSpec((tile_x, tile_y, 128), lambda i: (0, 0, 0)), ANY, ANY, ANY],
+        out_specs=(VM, VM, ANY, ANY, ANY, ANY),
         scratch_shapes=[
             pltpu.VMEM((peers, MSG, 128), f32),
             pltpu.VMEM((peers, ROWS, 128), f32),
-            pltpu.VMEM((columns, 128), bf16),
-            pltpu.VMEM((64, columns), f32),
+            pltpu.VMEM((256, 256), bf16),
+            pltpu.VMEM((256, 256), f32),
             pltpu.SemaphoreType.DMA,
             pltpu.SemaphoreType.DMA((peers,)),
             pltpu.SemaphoreType.DMA,
             pltpu.SemaphoreType.DMA,
+            pltpu.SemaphoreType.DMA((4,)),
+            pltpu.SemaphoreType.DMA((4,)),
         ],
-        compiler_params=pltpu.CompilerParams(has_side_effects=True, vmem_limit_bytes=48 << 20),
+        compiler_params=pltpu.CompilerParams(has_side_effects=True, vmem_limit_bytes=60 << 20),
         name="exchange",
-    )(msg, state)
+    )(msg, state, state, jnp.zeros((1, tile_y, width), f32), jnp.zeros((tile_x, 1, width), f32))
 
 
 def unpack_kernel(flat, back, stream_t, out, buf, rows):
@@ -306,11 +374,12 @@
 
 
 XB = 8
+PART = 8
 
 
 def columns_kernel(
     st, up, dn, x_low, x_high, y_low, y_high, lat, count, diff, scale, source, left, right, stoich_t,
-    out, w_first, w_low, s_high, s_low, lat_col, count_col, scale_col, rhs, coef, iface,
+    out, w_a, w_b, s_both, s_high, lat_col, count_col, scale_col, rhs, coef, iface,
 ):
     i = pl.program_id(0)
     last = pl.num_programs(0) - 1
@@ -318,19 +387,21 @@
 
     @pl.when(i == 0)
     def _():
+        inside = iota((64, 128), 0) // 32 == iota((64, 128), 1) // 64
+
+        def spread(w):
+            return jnp.where(inside, jnp.concatenate([jnp.concatenate([w] * 2, axis=1)] * 2, axis=0), 0.0)
+
+        pair = jnp.concatenate([spread(left[...]), spread(right[...])], axis=1)
+        high, low = split(pair)
+        none = jnp.zeros((64, 256), bf16)
+        w_a[...] = jnp.concatenate([high, high, low, none], axis=0)
+        w_b[...] = jnp.concatenate([high, high, none, low], axis=0)
         inside = iota((128, 256), 0) // 32 == iota((128, 256), 1) // 64
-
-        def spread(w):
-            wide = jnp.concatenate([w] * 4, axis=1)
-            return jnp.where(inside, jnp.concatenate([wide] * 4, axis=0), 0.0)
-
-        high, low = split(jnp.concatenate([spread(left[...]), spread(right[...])], axis=1))
-        w_first[0:128, :] = high
-        w_first[128:256, :] = high
-        w_low[...] = low
-        high, low = split(spread(stoich_t[...]).T)
+        wide = jnp.concatenate([stoich_t[...]] * 4, axis=1)
+        high, low = split(jnp.where(inside, jnp.concatenate([wide] * 4, axis=0), 0.0).T)
+        s_both[...] = jnp.concatenate([high, low], axis=1)
         s_high[...] = high
-        s_low[...] = low
 
         def turned(a):
             a = jnp.concatenate([a, jnp.zeros((32, 96), f32)], axis=1)
@@ -408,21 +479,34 @@
         high = rhs[cell(m), :] + coef[cell(m), :] * high
         rhs[cell(m), :] = high
 
+    half = lane < 64
     for cb in range(2):
         counts = jnp.concatenate(
             [jnp.broadcast_to(count_col[i, :, x : x + 1], (32, 128)) for x in range(4 * cb, 4 * cb + 4)], axis=0
         )
         depth = counts - (lane // 32).astype(f32)
-        for j in range(16):
-            at = slice(128 * j, 128 * j + 128)
-            x = rhs[at, 128 * cb : 128 * cb + 128].T
-            high, low = split(x)
-            both = dot(jnp.concatenate([high, low], axis=1), w_first[...]) + dot(high, w_low[...])
-            high, low = split(both[:, 0:256] * both[:, 256:512])
-            change = dot(high, s_high[...]) + dot(low, s_high[...]) + dot(high, s_low[...])
-            new = x + jnp.where(depth > 4.0 * j, 0.1, 0.0) * change
-            for p in range(4):
-                out[4 * cb + p, :, at] = new[32 * p : 32 * p + 32, :]
+        for first in range(0, 16, PART):
+            solved, pair_a, pair_b = [], [], []
+            for j in range(first, first + PART):
+                x = rhs[128 * j : 128 * j + 128, 128 * cb : 128 * cb + 128].T
+                high = x.astype(bf16)
+                wide = high.astype(f32)
+                low = pltpu.roll(x - wide, 64, axis=1)
+                pair_a.append(jnp.concatenate([jnp.where(half, wide, low).astype(bf16), high], axis=1))
+                pair_b.append(jnp.concatenate([jnp.where(half, low, wide).astype(bf16), high], axis=1))
+                solved.append(x)
+            both = dot(jnp.concatenate(pair_a, axis=0), w_a[...])
+            rates_a = split(both[:, 0:128] * both[:, 128:256])
+            both = dot(jnp.concatenate(pair_b, axis=0), w_b[...])
+            rates_b = split(both[:, 0:128] * both[:, 128:256])
+            change = dot(jnp.concatenate([rates_a[0], rates_b[0]], axis=1), s_both[...])
+            change = change[:, 0:128] + change[:, 128:256]
+            change = change + dot(jnp.concatenate([rates_a[1], rates_b[1]], axis=1), s_high[...])
+            for n in range(PART):
+                j = first + n
+                new = solved[n] + jnp.where(depth > 4.0 * j, 0.1, 0.0) * change[128 * n : 128 * n + 128, :]
+                for p in range(4):
+                    out[4 * cb + p, :, 128 * j : 128 * j + 128] = new[32 * p : 32 * p + 32, :]
 
 
 def columns(state, x_low, x_high, y_low, y_high, lat, count, diffusion, scale, source, left, right, stoich_t):
@@ -452,9 +536,9 @@
         ],
         out_specs=pl.BlockSpec((XB, tile_y, width), lambda i: (i, 0, 0)),
         scratch_shapes=[
-            pltpu.VMEM((256, 512), bf16),
-            pltpu.VMEM((128, 512), bf16),
-            pltpu.VMEM((256, 128), bf16),
+            pltpu.VMEM((256, 256), bf16),
+            pltpu.VMEM((256, 256), bf16),
+            pltpu.VMEM((256, 256), bf16),
             pltpu.VMEM((256, 128), bf16),
             pltpu.VMEM((steps, 32, 128), f32),
             pltpu.VMEM((steps, 32, 128), f32),
@@ -466,18 +550,6 @@
         compiler_params=pltpu.CompilerParams(vmem_limit_bytes=56 << 20),
         name="columns",
     )(state, state, state, x_low, x_high, y_low, y_high, lat, count, diffusion, scale, source, left, right, stoich_t)
-
-
-def halo(state):
-    out = []
-    for axis, dim in (("gx", 0), ("gy", 1)):
-        count = lax.axis_size(axis)
-        forward = [(i, i + 1) for i in range(count - 1)]
-        backward = [(target, source) for source, target in forward]
-        end = state.shape[dim] - 1
-        out.append(lax.ppermute(lax.slice_in_dim(state, end, end + 1, axis=dim), axis, forward))
-        out.append(lax.ppermute(lax.slice_in_dim(state, 0, 1, axis=dim), axis, backward))
-    return out
 
 
 def body(
@@ -495,12 +567,11 @@
     stoich,
 ):
     peers = lax.axis_size("gx") * lax.axis_size("gy")
-    x_low, x_high, y_low, y_high = halo(state)
     stream_t = stream.T
     flat, msg = pack(
         reach_owner.reshape(-1, 128), reach_local.reshape(-1, 128), exch_coef.reshape(-1, 128), stream_t, peers
     )
-    source, back = exchange(msg, state)
+    source, back, x_low, x_high, y_low, y_high = exchange(msg, state)
     state_out = columns(
         state, x_low, x_high, y_low, y_high, lat_coef, layer_count, diffusion, species_scale[None, :], source,
         rate_left, rate_right, stoich.T,

time: 158 us -> 118 us (0.75)
  the two profiles are of different devices: /device:TPU:1 before, /device:TPU:7 now
where the time goes in v1:
time: 118 us; the launch traced here: 117 us
  Pallas kernels  109 us (92%)
  local copies, waits for them, and re-layouts  7.11 us (6%)
    pallas_call x1, Pallas kernels, exchange(): pl.pallas_call(exchange_kernel, grid=(1,), out_shape=(jax.ShapeDtypeStruc...  61.8 us
    pallas_call x1, Pallas kernels, columns(): pl.pallas_call(columns_kernel, grid=(steps,), out_shape=jax.ShapeDtypeStr...  25 us
    pallas_call x1, Pallas kernels, pack(): pl.pallas_call(pack_kernel, out_shape=(jax.ShapeDtypeStruct((groups, 128)...  12.5 us
    pallas_call x1, Pallas kernels, unpack(): pl.pallas_call(unpack_kernel, out_shape=jax.ShapeDtypeStruct(stream_t.sha...  10.1 us
    unnamed x14, local copies, waits for them, and re-layouts  5.55 us

profile of v1, /device:TPU:7, one launch (start us, length us, event | category | flops | bytes accessed | tf_op | source)
XLA Modules:
  0.0 117.3 jit_solution(16612833159001004668)
XLA Ops:
  0.6 0.0 copy-start
  0.6 1.0 copy-done
  1.7 0.0 copy-start.4
  1.7 0.7 copy-done.4
  2.4 0.0 copy-start.5
  2.4 0.7 copy-done.5
  3.1 0.0 copy-start.6
  3.1 0.7 copy-done.6
  3.8 12.5 %pack.1 = (s32[32,128]{1,0:T(8,128)S(1)}, f32[128,17,128]{2,1,0:T(8,128)S(1)}) custom-call(s32[32,128]{1,0:T(8,128)S(1)} %bitcast.9, s32[32,128]{1,0:T(8,128)S(1)} %bitcast.10, f32[32,128]{1,0:T(8,128)S(1)} %bitcast.11, f32[32,4096]{1,0:T(8,128)S(1)} %bitcast.7), custom_call_target="tpu_custom_call" | custom-call | tf_op jit(solution)/shard_map/pack/pallas_call | solution.py:110
  16.4 0.0 copy-start.2
  16.4 1.1 copy-done.2
  17.5 0.8 broadcast_in_dim.10.none_y
  18.4 0.7 broadcast_in_dim.9.none_x
  19.1 0.0 copy-start.1
  19.1 61.8 %exchange.1 = (f32[32,1024]{1,0:T(8,128)}, f32[128,16,128]{2,1,0:T(8,128)}, f32[1,32,2048]{2,1,0:T(8,128)}, f32[1,32,2048]{2,1,0:T(8,128)}, f32[32,1,2048]{2,1,0:T(1,128)}, /*index=5*/f32[32,1,2048]{2,1,0:T(1,128)}) custom-call(f32[128,17,128]{2,1,0:T(8,128)} %copy-done.2, f32[32,32,2048]{2,1,0:T(8,128)} %dn.1, f32[32,32,2048]{2,1,0:T(8,128)} %dn.1, ...), custom_call_target="tpu_custom_call" | custom-call | tf_op jit(solution)/shard_map/exchange/pallas_call | solution.py:310
  80.9 0.0 copy-done.1
  80.9 0.0 copy-start.3
  80.9 1.2 %copy-done.3 = f32[128,16,128]{2,1,0:T(8,128)S(1)} copy-done((f32[128,16,128]{2,1,0:T(8,128)S(1)}, f32[128,16,128]{2,1,0:T(8,128)}, u32[]{:S(2)}) %copy-start.3) | copy-done | bytes 1048600
  82.2 10.1 %unpack.1 = f32[32,4096]{1,0:T(8,128)} custom-call(s32[32,128]{1,0:T(8,128)S(1)} %get-tuple-element.16.flat, f32[128,16,128]{2,1,0:T(8,128)S(1)} %copy-done.3, f32[32,4096]{1,0:T(8,128)S(1)} %bitcast.8), custom_call_target="tpu_custom_call" | custom-call | tf_op jit(solution)/shard_map/unpack/pallas_call | solution.py:365
  92.3 25.0 %columns.1 = f32[32,32,2048]{2,1,0:T(8,128)} custom-call(f32[32,32,2048]{2,1,0:T(8,128)} %dn.1, f32[32,32,2048]{2,1,0:T(8,128)} %dn.1, f32[32,32,2048]{2,1,0:T(8,128)} %dn.1, f32[1,32,2048]{2,1,0:T(8,128)} %get-tuple-element.11.x_low, f32[1,32,2048]{2,1,0:T(8,128)} %get-tuple-element.12.x_high, f32[32,1,2048]{2,1,0:T(1,128)} %get-tuple-element.13.y_low, ...), custom_call_target="tpu_custom_call" | custom-call | tf_op jit(solution)/shard_map/columns/pallas_call | solution.py:516
Async XLA Ops:
  0.6 1.0 copy-start
  1.7 0.7 copy-start.4
  2.4 0.7 copy-start.5
  3.1 0.7 copy-start.6
  16.4 1.1 copy-start.2
  19.1 61.9 %copy-start.1 = (f32[4096,32]{0,1:T(8,128)S(1)}, f32[4096,32]{0,1:T(8,128)}, u32[]{:S(2)}) copy-start(f32[4096,32]{0,1:T(8,128)} %param.17) | copy-start | bytes 1572868
  80.9 1.2 %copy-start.3 = (f32[128,16,128]{2,1,0:T(8,128)S(1)}, f32[128,16,128]{2,1,0:T(8,128)}, u32[]{:S(2)}) copy-start(f32[128,16,128]{2,1,0:T(8,128)} %get-tuple-element.17.back) | copy-start | bytes 3145732

commit v2 on v1

--- a/solution.py
+++ b/solution.py
@@ -16,7 +16,7 @@
 ROWS = 16
 MSG = ROWS + 1
 FORM = 16
-BATCH = 8
+BATCH = 16
 
 
 def iota(shape, dim):
@@ -196,18 +196,111 @@
         source[:, 256 * g : 256 * g + 256] = acc[64 * g : 64 * g + 32, :] + acc[64 * g + 32 : 64 * g + 64, :]
 
 
+def prepare(st, y_low, y_high, lat_col, count, diff, rhs, iface):
+    row = iota((32, 128), 0)
+
+    def step(cb, _):
+        block, lanes = cb // 2, pl.ds(pl.multiple_of(lax.rem(cb, 2) * 128, 128), 128)
+        lats = [jnp.broadcast_to(lat_col[cb, :, x : x + 1], (32, 128)) for x in range(4)]
+        for j in range(16):
+            at = slice(128 * j, 128 * j + 128)
+            parts = []
+            for x in range(4):
+                here = 4 * cb + x
+                s = st[here + 1, :, at]
+                lower = jnp.where(row == 0, y_low[here, :, at], pltpu.roll(s, 1, axis=0))
+                upper = jnp.where(row == 31, y_high[here, :, at], pltpu.roll(s, 31, axis=0))
+                beside = (st[here, :, at] + st[here + 2, :, at]) + (lower + upper)
+                parts.append(s + lats[x] * (beside - 4.0 * s))
+            rhs[block, at, lanes] = jnp.concatenate(parts, axis=0).T
+        counts = jnp.concatenate([count[pl.ds(4 * cb + x, 1), :] for x in range(4)], axis=1)
+        d = diff[pl.ds(4 * cb, 4)].reshape(128, 64)
+        d = jnp.concatenate([d, jnp.zeros((128, 64), f32)], axis=1).T[0:64, :]
+        iface[block, :, lanes] = jnp.where(iota((64, 128), 0) + 1 < counts, d, 0.0)
+        return 0
+
+    lax.fori_loop(0, 8, step, 0)
+
+
+def eliminate(rhs, coef, iface, scale_col, block):
+    scales = jnp.concatenate([scale_col[...]] * 4, axis=1)
+
+    def cell(k):
+        return pl.ds(32 * k, 32)
+
+    def put(ref, k, value):
+        ref[block, cell(k), :] = value[:, 0:256]
+        ref[block + 1, cell(k), :] = value[:, 256:512]
+
+    def get(k):
+        return jnp.concatenate([rhs[block, cell(k), :], rhs[block + 1, cell(k), :]], axis=1)
+
+    def layers(n, carry):
+        c, d, u = carry
+        for m in range(7):
+            k = 63 - 7 * n - m
+            v = scales * jnp.concatenate([iface[block, pl.ds(k - 1, 1), :], iface[block + 1, pl.ds(k - 1, 1), :]], axis=1)
+            r = 1.0 / (1.0 + v + u * (1.0 - c))
+            d = (get(k) + u * d) * r
+            c = v * r
+            u = v
+            put(rhs, k, d)
+            put(coef, k, c)
+        return c, d, u
+
+    zero = jnp.zeros((32, 512), f32)
+    c, d, u = lax.fori_loop(0, 9, layers, (zero, zero, zero))
+    r = 1.0 / (1.0 + u * (1.0 - c))
+    put(rhs, 0, (get(0) + u * d) * r)
+    put(coef, 0, r)
+
+
 def exchange_kernel(
-    msg, state_top, state, none_x, none_y, source, back, x_low, x_high, y_low, y_high,
-    inbox, outbox, top, acc, send1, recv1, send2, recv2, send_edge, recv_edge,
+    msg, state, lat, count, diff, scale, source, back, rhs_out, coef_out,
+    st, y_low, y_high, rhs, coef, iface, lat_col, scale_col, inbox, outbox, top, acc,
+    send1, recv1, send2, recv2, send_edge, recv_edge, local,
 ):
     peers = msg.shape[0]
-    size_x = lax.axis_size("gx")
-    ends = state.shape[0] - 1, state.shape[1] - 1
-    size_y = lax.axis_size("gy")
-    me = lax.axis_index("gx") * size_y + lax.axis_index("gy")
+    size_x, size_y = lax.axis_size("gx"), lax.axis_size("gy")
+    gx, gy = lax.axis_index("gx"), lax.axis_index("gy")
+    me = gx * size_y + gy
+    tile_x, tile_y, _ = state.shape
 
     def device(t):
         return (t // size_y, lax.rem(t, size_y))
+
+    barrier = pltpu.get_barrier_semaphore()
+
+    def greet(d, _):
+        pl.semaphore_signal(barrier, inc=1, device_id=device(lax.rem(me + d, peers)), device_id_type=MESH)
+        return 0
+
+    lax.fori_loop(1, peers, greet, 0)
+    load = pltpu.make_async_copy(state, st.at[pl.ds(1, tile_x)], local.at[0])
+    load.start()
+
+    edges = [
+        (state.at[pl.ds(tile_x - 1, 1)], st.at[pl.ds(0, 1)], (lax.rem(gx + 1, size_x), gy), gx < size_x - 1, gx > 0),
+        (state.at[pl.ds(0, 1)], st.at[pl.ds(tile_x + 1, 1)], (lax.rem(gx + size_x - 1, size_x), gy), gx > 0, gx < size_x - 1),
+        (state.at[:, pl.ds(tile_y - 1, 1)], y_low, (gx, lax.rem(gy + 1, size_y)), gy < size_y - 1, gy > 0),
+        (state.at[:, pl.ds(0, 1)], y_high, (gx, lax.rem(gy + size_y - 1, size_y)), gy > 0, gy < size_y - 1),
+    ]
+
+    def edge(n):
+        block, to, device_id, _, _ = edges[n]
+        return pltpu.make_async_remote_copy(
+            src_ref=block,
+            dst_ref=to,
+            send_sem=send_edge.at[n],
+            recv_sem=recv_edge.at[n],
+            device_id=device_id,
+            device_id_type=MESH,
+        )
+
+    for n in range(4):
+        @pl.when(jnp.logical_not(edges[n][4]))
+        def _():
+            edges[n][1][...] = jnp.zeros(edges[n][1].shape, f32)
 
     def send(d):
         to = lax.rem(me + d, peers)
@@ -231,41 +324,42 @@
             device_id_type=MESH,
         )
 
-    gx, gy = lax.axis_index("gx"), lax.axis_index("gy")
-    edges = [
-        (state.at[pl.ds(ends[0], 1)], x_low, (lax.rem(gx + 1, size_x), gy), gx < size_x - 1, gx > 0),
-        (state.at[pl.ds(0, 1)], x_high, (lax.rem(gx + size_x - 1, size_x), gy), gx > 0, gx < size_x - 1),
-        (state.at[:, pl.ds(ends[1], 1)], y_low, (gx, lax.rem(gy + 1, size_y)), gy < size_y - 1, gy > 0),
-        (state.at[:, pl.ds(0, 1)], y_high, (gx, lax.rem(gy + size_y - 1, size_y)), gy > 0, gy < size_y - 1),
-    ]
-
-    def edge(n):
-        block, to, device_id, _, _ = edges[n]
-        return pltpu.make_async_remote_copy(
-            src_ref=block,
-            dst_ref=to,
-            send_sem=send_edge.at[n],
-            recv_sem=recv_edge.at[n],
-            device_id=device_id,
-            device_id_type=MESH,
-        )
-
-    def outside(n):
-        return pltpu.make_async_copy(none_x if n < 2 else none_y, edges[n][1], recv_edge.at[n])
-
     def start(d, _):
         send(d).start()
         return 0
 
-    lax.fori_loop(1, peers, start, 0)
+    pl.semaphore_wait(barrier, peers - 1)
     for n in range(4):
         pl.when(edges[n][3])(edge(n).start)
-        pl.when(jnp.logical_not(edges[n][4]))(outside(n).start)
+    lax.fori_loop(1, peers, start, 0)
     keep = pltpu.make_async_copy(msg.at[me], inbox.at[0], recv1.at[0])
     keep.start()
-    columns = state_top.shape[0] * state_top.shape[1]
-    top_of(state_top[...].reshape(columns, 128), top)
+
+    lat_t = jnp.concatenate([lat[...], jnp.zeros((32, 96), f32)], axis=1)
+    lat_t = jnp.concatenate([lat_t, jnp.zeros((96, 128), f32)], axis=0).T
+    for g in range(8):
+        lat_col[g] = pltpu.roll(lat_t, (128 - 4 * g) % 128, axis=1)[0:32, :]
+    scale_col[...] = jnp.broadcast_to(
+        jnp.sum(
+            jnp.where(iota((32, 32), 0) == iota((32, 32), 1), jnp.broadcast_to(scale[...], (32, 32)), 0.0),
+            axis=1,
+            keepdims=True,
+        ),
+        (32, 128),
+    )
     acc[...] = jnp.zeros_like(acc)
+    load.wait()
+    top_of(st[1 : tile_x + 1, :, 0:128].reshape(tile_x * tile_y, 128), top)
+    for n in range(4):
+        pl.when(edges[n][4])(edge(n).wait_recv)
+    prepare(st, y_low, y_high, lat_col, count, diff, rhs, iface)
+    saved = []
+    for block in (0, 2):
+        eliminate(rhs, coef, iface, scale_col, block)
+        for n, (made, to) in enumerate(((rhs, rhs_out), (coef, coef_out))):
+            two = pl.ds(block, 2)
+            saved.append(pltpu.make_async_copy(made.at[two], to.at[two], local.at[1 + block + n]))
+            saved[-1].start()
     keep.wait()
 
     def work(c, first):
@@ -294,33 +388,37 @@
     own.wait()
     for n in range(4):
         pl.when(edges[n][3])(edge(n).wait_send)
-        pl.when(edges[n][4])(edge(n).wait_recv)
-        pl.when(jnp.logical_not(edges[n][4]))(outside(n).wait)
+    for copy in saved:
+        copy.wait()
     rest = pl.ds(0, peers - 1)
     pltpu.make_async_copy(msg.at[rest], msg.at[rest], send1).wait()
     pltpu.make_async_copy(outbox.at[rest], outbox.at[rest], send2).wait()
     pltpu.make_async_copy(back.at[rest], back.at[rest], recv2).wait()
 
 
-def exchange(msg, state):
+def exchange(msg, state, lat, count, diffusion, scale):
     peers = msg.shape[0]
     tile_x, tile_y, width = state.shape
-    edge_x = jax.ShapeDtypeStruct((1, tile_y, width), f32)
-    edge_y = jax.ShapeDtypeStruct((tile_x, 1, width), f32)
+    solve = jax.ShapeDtypeStruct((4, width, 256), f32)
     return pl.pallas_call(
         exchange_kernel,
-        grid=(1,),
         out_shape=(
             jax.ShapeDtypeStruct((32, tile_x * tile_y), f32),
             jax.ShapeDtypeStruct((peers, ROWS, 128), f32),
-            edge_x,
-            edge_x,
-            edge_y,
-            edge_y,
+            solve,
+            solve,
         ),
-        in_specs=[VM, pl.BlockSpec((tile_x, tile_y, 128), lambda i: (0, 0, 0)), ANY, ANY, ANY],
-        out_specs=(VM, VM, ANY, ANY, ANY, ANY),
+        in_specs=[ANY, ANY, VM, VM, VM, VM],
+        out_specs=(VM, ANY, ANY, ANY),
         scratch_shapes=[
+            pltpu.VMEM((tile_x + 2, tile_y, width), f32),
+            pltpu.VMEM((tile_x, 1, width), f32),
+            pltpu.VMEM((tile_x, 1, width), f32),
+            pltpu.VMEM((4, width, 256), f32),
+            pltpu.VMEM((4, width, 256), f32),
+            pltpu.VMEM((4, 64, 256), f32),
+            pltpu.VMEM((8, 32, 128), f32),
+            pltpu.VMEM((32, 128), f32),
             pltpu.VMEM((peers, MSG, 128), f32),
             pltpu.VMEM((peers, ROWS, 128), f32),
             pltpu.VMEM((256, 256), bf16),
@@ -331,10 +429,11 @@
             pltpu.SemaphoreType.DMA,
             pltpu.SemaphoreType.DMA((4,)),
             pltpu.SemaphoreType.DMA((4,)),
+            pltpu.SemaphoreType.DMA((5,)),
         ],
-        compiler_params=pltpu.CompilerParams(has_side_effects=True, vmem_limit_bytes=60 << 20),
+        compiler_params=pltpu.CompilerParams(collective_id=0, has_side_effects=True, vmem_limit_bytes=58 << 20),
         name="exchange",
-    )(msg, state, state, jnp.zeros((1, tile_y, width), f32), jnp.zeros((tile_x, 1, width), f32))
+    )(msg, state, lat, count, diffusion, scale)
 
 
 def unpack_kernel(flat, back, stream_t, out, buf, rows):
@@ -342,13 +441,14 @@
     peers = back.shape[0]
 
     def spread(t, _):
-        m = back[t]
-        at = pl.multiple_of(t * CAP, CAP)
-        for q in range(4):
-            buf[pl.ds(at + 16 * q, 16), :] = pltpu.roll(m, 128 - 32 * q, axis=1) if q else m
-        return 0
-
-    lax.fori_loop(0, peers, spread, 0, unroll=4)
+        m = back[pl.ds(pl.multiple_of(t * FORM, FORM), FORM)].reshape(FORM * 16, 128)
+        parts = [m] + [pltpu.roll(m, 128 - 32 * q, axis=1) for q in range(1, 4)]
+        parts = [p.reshape(FORM, 1, 16, 128) for p in parts]
+        at = pl.multiple_of(t * FORM * CAP, FORM * CAP)
+        buf[pl.ds(at, FORM * CAP), :] = jnp.concatenate(parts, axis=1).reshape(FORM * CAP, 128)
+        return 0
+
+    lax.fori_loop(0, peers // FORM, spread, 0)
 
     def move(g, _):
         at = pl.multiple_of(g * 128, 128)
@@ -377,13 +477,9 @@
 PART = 8
 
 
-def columns_kernel(
-    st, up, dn, x_low, x_high, y_low, y_high, lat, count, diff, scale, source, left, right, stoich_t,
-    out, w_a, w_b, s_both, s_high, lat_col, count_col, scale_col, rhs, coef, iface,
-):
+def columns_kernel(rhs, coef, count, source, left, right, stoich_t, out, w_a, w_b, s_both, s_high, count_col, solved_t):
     i = pl.program_id(0)
-    last = pl.num_programs(0) - 1
-    sub, lane = iota((128, 128), 0), iota((128, 128), 1)
+    lane = iota((128, 128), 1)
 
     @pl.when(i == 0)
     def _():
@@ -402,82 +498,17 @@
         high, low = split(jnp.where(inside, jnp.concatenate([wide] * 4, axis=0), 0.0).T)
         s_both[...] = jnp.concatenate([high, low], axis=1)
         s_high[...] = high
-
-        def turned(a):
-            a = jnp.concatenate([a, jnp.zeros((32, 96), f32)], axis=1)
-            return jnp.concatenate([a, jnp.zeros((96, 128), f32)], axis=0).T
-
-        lat_t, count_t = turned(lat[...]), turned(count[...].astype(f32))
+        turned = jnp.concatenate([count[...].astype(f32), jnp.zeros((32, 96), f32)], axis=1)
+        turned = jnp.concatenate([turned, jnp.zeros((96, 128), f32)], axis=0).T
         for g in range(4):
-            lat_col[g] = pltpu.roll(lat_t, (128 - XB * g) % 128, axis=1)[0:32, :]
-            count_col[g] = pltpu.roll(count_t, (128 - XB * g) % 128, axis=1)[0:32, :]
-        scale_col[...] = jnp.broadcast_to(
-            jnp.sum(
-                jnp.where(iota((32, 32), 0) == iota((32, 32), 1), jnp.broadcast_to(scale[...], (32, 32)), 0.0),
-                axis=1,
-                keepdims=True,
-            ),
-            (32, 128),
-        )
-
-    row = iota((32, 128), 0)
-    lats = [jnp.broadcast_to(lat_col[i, :, x : x + 1], (32, 128)) for x in range(XB)]
-    for cb in range(2):
-        for j in range(16):
-            at = slice(128 * j, 128 * j + 128)
-            parts = []
-            for x in range(4 * cb, 4 * cb + 4):
-                s = st[x, :, at]
-                before = st[x - 1, :, at] if x else jnp.where(i == 0, x_low[0, :, at], up[0, :, at])
-                after = st[x + 1, :, at] if x < XB - 1 else jnp.where(i == last, x_high[0, :, at], dn[0, :, at])
-                lower = jnp.where(row == 0, y_low[x, :, at], pltpu.roll(s, 1, axis=0))
-                upper = jnp.where(row == 31, y_high[x, :, at], pltpu.roll(s, 31, axis=0))
-                parts.append(s + lats[x] * ((before + after) + (lower + upper) - 4.0 * s))
-            rhs[at, 128 * cb : 128 * cb + 128] = jnp.concatenate(parts, axis=0).T
-        counts = jnp.concatenate([count[pl.ds(XB * i + 4 * cb + x, 1), :] for x in range(4)], axis=1)
-        d = diff[4 * cb : 4 * cb + 4].reshape(128, 64)
-        d = jnp.concatenate([d, jnp.zeros((128, 64), f32)], axis=1).T[0:64, :]
-        iface[:, 128 * cb : 128 * cb + 128] = jnp.where(iota((64, 128), 0) + 1 < counts, d, 0.0)
-    rhs[0:32, :] += source[...]
-
-    scales = jnp.concatenate([scale_col[...]] * 2, axis=1)
-    zero = jnp.zeros((32, 256), f32)
-
-    def upper_at(k):
-        return scales * iface[k : k + 1, :]
-
-    def cell(k):
-        return slice(32 * k, 32 * k + 32)
-
-    c, d, u_before = zero, zero, zero
-    e_c, e_d, u_here = zero, zero, upper_at(63)
-    for k in range(32):
-        u = upper_at(k)
-        r = 1.0 / (1.0 + u + u_before * (1.0 - c))
-        d = (rhs[cell(k), :] + u_before * d) * r
-        c = u * r
-        u_before = u
-        m = 63 - k
-        v = upper_at(m - 1)
-        r = 1.0 / (1.0 + v + u_here * (1.0 - e_c))
-        e_d = (rhs[cell(m), :] + u_here * e_d) * r
-        e_c = v * r
-        u_here = v
-        if k < 31:
-            coef[cell(k), :] = c
-            rhs[cell(k), :] = d
-            coef[cell(m), :] = e_c
-            rhs[cell(m), :] = e_d
-    low = (d + c * e_d) / (1.0 - c * e_c)
-    high = e_d + e_c * low
-    rhs[cell(31), :] = low
-    rhs[cell(32), :] = high
-    for k in range(30, -1, -1):
-        low = rhs[cell(k), :] + coef[cell(k), :] * low
-        rhs[cell(k), :] = low
-        m = 63 - k
-        high = rhs[cell(m), :] + coef[cell(m), :] * high
-        rhs[cell(m), :] = high
+            count_col[g] = pltpu.roll(turned, (128 - XB * g) % 128, axis=1)[0:32, :]
+
+    x = rhs[0, 0:32, :] + coef[0, 0:32, :] * source[...]
+    solved_t[0:32, :] = x
+    for k in range(1, 64):
+        cell = slice(32 * k, 32 * k + 32)
+        x = rhs[0, cell, :] + coef[0, cell, :] * x
+        solved_t[cell, :] = x
 
     half = lane < 64
     for cb in range(2):
@@ -488,7 +519,7 @@
         for first in range(0, 16, PART):
             solved, pair_a, pair_b = [], [], []
             for j in range(first, first + PART):
-                x = rhs[128 * j : 128 * j + 128, 128 * cb : 128 * cb + 128].T
+                x = solved_t[128 * j : 128 * j + 128, 128 * cb : 128 * cb + 128].T
                 high = x.astype(bf16)
                 wide = high.astype(f32)
                 low = pltpu.roll(x - wide, 64, axis=1)
@@ -509,27 +540,19 @@
                     out[4 * cb + p, :, 128 * j : 128 * j + 128] = new[32 * p : 32 * p + 32, :]
 
 
-def columns(state, x_low, x_high, y_low, y_high, lat, count, diffusion, scale, source, left, right, stoich_t):
-    tile_x, tile_y, width = state.shape
-    steps = tile_x // XB
+def columns(rhs, coef, count, source, left, right, stoich_t):
+    tile_x, tile_y = count.shape
+    steps, width, _ = rhs.shape
     whole = lambda shape: pl.BlockSpec(shape, lambda i: (0,) * len(shape))
     return pl.pallas_call(
         columns_kernel,
         grid=(steps,),
-        out_shape=jax.ShapeDtypeStruct(state.shape, f32),
+        out_shape=jax.ShapeDtypeStruct((tile_x, tile_y, width), f32),
         in_specs=[
-            pl.BlockSpec((XB, tile_y, width), lambda i: (i, 0, 0)),
-            pl.BlockSpec((1, tile_y, width), lambda i: (jnp.maximum(XB * i - 1, 0), 0, 0)),
-            pl.BlockSpec((1, tile_y, width), lambda i: (jnp.minimum(XB * i + XB, tile_x - 1), 0, 0)),
-            whole(x_low.shape),
-            whole(x_high.shape),
-            pl.BlockSpec((XB, 1, width), lambda i: (i, 0, 0)),
-            pl.BlockSpec((XB, 1, width), lambda i: (i, 0, 0)),
-            whole(lat.shape),
+            pl.BlockSpec((1, width, 256), lambda i: (i, 0, 0)),
+            pl.BlockSpec((1, width, 256), lambda i: (i, 0, 0)),
             whole(count.shape),
-            pl.BlockSpec((XB, tile_y, diffusion.shape[2]), lambda i: (i, 0, 0)),
-            whole(scale.shape),
-            pl.BlockSpec((32, XB * tile_y), lambda i: (0, i)),
+            pl.BlockSpec((32, 256), lambda i: (0, i)),
             whole(left.shape),
             whole(right.shape),
             whole(stoich_t.shape),
@@ -541,15 +564,11 @@
             pltpu.VMEM((256, 256), bf16),
             pltpu.VMEM((256, 128), bf16),
             pltpu.VMEM((steps, 32, 128), f32),
-            pltpu.VMEM((steps, 32, 128), f32),
-            pltpu.VMEM((32, 128), f32),
-            pltpu.VMEM((width, XB * tile_y), f32),
-            pltpu.VMEM((width, XB * tile_y), f32),
-            pltpu.VMEM((64, XB * tile_y), f32),
+            pltpu.VMEM((width, 256), f32),
         ],
         compiler_params=pltpu.CompilerParams(vmem_limit_bytes=56 << 20),
         name="columns",
-    )(state, state, state, x_low, x_high, y_low, y_high, lat, count, diffusion, scale, source, left, right, stoich_t)
+    )(rhs, coef, count, source, left, right, stoich_t)
 
 
 def body(
@@ -571,11 +590,8 @@
     flat, msg = pack(
         reach_owner.reshape(-1, 128), reach_local.reshape(-1, 128), exch_coef.reshape(-1, 128), stream_t, peers
     )
-    source, back, x_low, x_high, y_low, y_high = exchange(msg, state)
-    state_out = columns(
-        state, x_low, x_high, y_low, y_high, lat_coef, layer_count, diffusion, species_scale[None, :], source,
-        rate_left, rate_right, stoich.T,
-    )
+    source, back, rhs, coef = exchange(msg, state, lat_coef, layer_count, diffusion, species_scale[None, :])
+    state_out = columns(rhs, coef, layer_count, source, rate_left, rate_right, stoich.T)
     stream_out = unpack(flat, back, stream_t).T
     return (state_out, stream_out)
 

time: 118 us -> 106 us (0.90)
  the two profiles are of different devices: /device:TPU:7 before, /device:TPU:1 now
where the time goes in v2:
time: 106 us
  Pallas kernels  101 us (95%)
  local copies, waits for them, and re-layouts  4.34 us (4%)
    pallas_call x1, Pallas kernels, exchange(): pl.pallas_call(exchange_kernel, out_shape=(jax.ShapeDtypeStruct((32, tile...  61.6 us
    pallas_call x1, Pallas kernels, columns(): pl.pallas_call(columns_kernel, grid=(steps,), out_shape=jax.ShapeDtypeStr...  18.4 us
    pallas_call x1, Pallas kernels, pack(): pl.pallas_call(pack_kernel, out_shape=(jax.ShapeDtypeStruct((groups, 128)...  12.5 us
    pallas_call x1, Pallas kernels, unpack(): pl.pallas_call(unpack_kernel, out_shape=jax.ShapeDtypeStruct(stream_t.sha...  8.52 us
    unnamed x14, local copies, waits for them, and re-layouts  4.34 us

profile of v2, /device:TPU:1, one launch (start us, length us, event | category | flops | bytes accessed | tf_op | source)
XLA Modules:
  0.0 106.1 jit_solution(10420007059172447336)
XLA Ops:
  0.6 0.0 copy-start
  0.6 1.0 copy-done
  1.7 0.0 copy-start.4
  1.7 0.7 copy-done.4
  2.4 0.0 copy-start.5
  2.4 0.7 copy-done.5
  3.1 0.0 copy-start.6
  3.1 0.7 copy-done.6
  3.8 12.5 %pack.1 = (s32[32,128]{1,0:T(8,128)S(1)}, f32[128,17,128]{2,1,0:T(8,128)S(1)}) custom-call(s32[32,128]{1,0:T(8,128)S(1)} %bitcast.9, s32[32,128]{1,0:T(8,128)S(1)} %bitcast.10, f32[32,128]{1,0:T(8,128)S(1)} %bitcast.11, f32[32,4096]{1,0:T(8,128)S(1)} %bitcast.7), custom_call_target="tpu_custom_call" | custom-call | tf_op jit(solution)/shard_map/pack/pallas_call | solution.py:110
  16.4 0.0 copy-start.2
  16.4 1.1 %copy-done.2 = f32[128,17,128]{2,1,0:T(8,128)} copy-done((f32[128,17,128]{2,1,0:T(8,128)}, f32[128,17,128]{2,1,0:T(8,128)S(1)}, u32[]{:S(2)}) %copy-start.2) | copy-done | bytes 1114136
  17.5 61.6 %exchange.1 = (f32[32,1024]{1,0:T(8,128)}, f32[128,16,128]{2,1,0:T(8,128)}, f32[4,2048,256]{2,1,0:T(8,128)}, f32[4,2048,256]{2,1,0:T(8,128)}) custom-call(f32[128,17,128]{2,1,0:T(8,128)} %copy-done.2, f32[32,32,2048]{2,1,0:T(8,128)} %state.1, f32[32,32]{1,0:T(8,128)} %lat.1, s32[32,32]{1,0:T(8,128)} %count.3, f32[32,32,64]{2,1,0:T(8,128)} %diff.1, ...), custom_call_target="tpu_custom_call" | custom-call | tf_op jit(solution)/shard_map/exchange/pallas_call | solution.py:403
  79.1 0.0 copy-start.1
  79.1 0.0 copy-start.3
  79.1 18.4 %columns.1 = f32[32,32,2048]{2,1,0:T(8,128)} custom-call(f32[4,2048,256]{2,1,0:T(8,128)} %get-tuple-element.9.rhs, f32[4,2048,256]{2,1,0:T(8,128)} %get-tuple-element.10.coef, s32[32,32]{1,0:T(8,128)} %count.3, f32[32,1024]{1,0:T(8,128)} %get-tuple-element.11.source, f32[32,64]{1,0:T(8,128)} %left.1, f32[32,64]{1,0:T(8,128)} %right.1, f32[32,64]{1,0:T(8,128)} %bitcast.13), custom_call_target="tpu_custom_call" | custom-call | tf_op jit(solution)/shard_map/columns/pallas_call | solution.py:547
  97.6 0.0 copy-done.1
  97.6 0.0 copy-done.3
  97.6 8.5 %unpack.1 = f32[32,4096]{1,0:T(8,128)} custom-call(s32[32,128]{1,0:T(8,128)S(1)} %get-tuple-element.12.flat, f32[128,16,128]{2,1,0:T(8,128)S(1)} %copy-done.3, f32[32,4096]{1,0:T(8,128)S(1)} %bitcast.8), custom_call_target="tpu_custom_call" | custom-call | tf_op jit(solution)/shard_map/unpack/pallas_call | solution.py:465
Async XLA Ops:
  0.6 1.0 copy-start
  1.7 0.7 copy-start.4
  2.4 0.7 copy-start.5
  3.1 0.7 copy-start.6
  16.4 1.1 %copy-start.2 = (f32[128,17,128]{2,1,0:T(8,128)}, f32[128,17,128]{2,1,0:T(8,128)S(1)}, u32[]{:S(2)}) copy-start(f32[128,17,128]{2,1,0:T(8,128)S(1)} %get-tuple-element.8.msg) | copy-start | bytes 3342340
  79.1 18.4 %copy-start.1 = (f32[4096,32]{0,1:T(8,128)S(1)}, f32[4096,32]{0,1:T(8,128)}, u32[]{:S(2)}) copy-start(f32[4096,32]{0,1:T(8,128)} %param.17) | copy-start | bytes 1572868
  79.1 18.4 %copy-start.3 = (f32[128,16,128]{2,1,0:T(8,128)S(1)}, f32[128,16,128]{2,1,0:T(8,128)}, u32[]{:S(2)}) copy-start(f32[128,16,128]{2,1,0:T(8,128)} %get-tuple-element.13.back) | copy-start | bytes 3145732

commit v3 on v2

v3 whole, which is shorter than its diff:
```python
import functools

import jax
import jax.numpy as jnp
from jax import lax
from jax.experimental import pallas as pl
from jax.experimental.pallas import tpu as pltpu
from jax.sharding import PartitionSpec as P

MESH = pl.DeviceIdType.MESH
f32, bf16, i32 = jnp.float32, jnp.bfloat16, jnp.int32
VM = pl.BlockSpec(memory_space=pltpu.VMEM)
ANY = pl.BlockSpec(memory_space=pl.ANY)

CAP = 64
ROWS = 16
MSG = ROWS + 1
FORM = 16
BATCH = 16


def iota(shape, dim):
    return lax.broadcasted_iota(i32, shape, dim)


def split(x):
    hi = x.astype(bf16)
    return hi, (x - hi.astype(f32)).astype(bf16)


def dot(a, b):
    return jnp.dot(a, b, preferred_element_type=f32)


def pack_kernel(owner, local, coef, stream_t, flat_out, msg, rows, buf, flat_v, flat_s, sem):
    groups = owner.shape[0]
    peers = msg.shape[0]
    sub, lane = iota((128, 128), 0), iota((128, 128), 1)
    upto = (sub <= lane).astype(bf16)
    ones = jnp.ones((128, 128), bf16)
    carry = jnp.zeros((128, 128), f32)
    for g in range(groups):
        mine = sub == owner[g : g + 1, :]
        onehot = mine.astype(f32).astype(bf16)
        count = dot(onehot, upto) + carry
        carry = carry + dot(onehot, ones)
        rank = jnp.sum(jnp.where(mine, count, 0.0), axis=0, keepdims=True)
        flat_v[g : g + 1, :] = owner[g : g + 1, :] * CAP + rank.astype(i32) - 1
    pltpu.make_async_copy(flat_v, flat_s, sem).start()
    flat_out[...] = flat_v[...]

    def fill(g, _):
        at = pl.multiple_of(g * 128, 128)
        block = jnp.concatenate(
            [
                stream_t[:, pl.ds(at, 128)],
                local[pl.ds(g, 1), :].astype(f32),
                coef[pl.ds(g, 1), :],
                jnp.zeros((94, 128), f32),
            ],
            axis=0,
        )
        rows[pl.ds(at, 128), :] = block.T
        return 0

    lax.fori_loop(0, groups, fill, 0)
    empty = jnp.where(lane == 32, -1.0, 0.0)

    def clear(g, _):
        buf[pl.ds(pl.multiple_of(g * 128, 128), 128), :] = empty
        return 0

    lax.fori_loop(0, buf.shape[0] // 128, clear, 0)
    pltpu.make_async_copy(flat_v, flat_s, sem).wait()

    def move(g, _):
        for j in range(128):
            buf[pl.ds(flat_s[g, j], 1), :] = rows[pl.ds(g * 128 + j, 1), :]
        return 0

    lax.fori_loop(0, groups, move, 0)
    lanes = iota((FORM * 16, 128), 1)
    spot = lanes // 8 == (16 - iota((FORM * 16, 128), 0) % 16) % 16

    def form(t, _):
        at = pl.multiple_of(t * FORM * CAP, FORM * CAP)
        part = buf[pl.ds(at, FORM * CAP), :].reshape(FORM, 4, 16, 128)
        part = [part[:, q].reshape(FORM * 16, 128) for q in range(4)]
        vals = pltpu.roll(part[3], 96, axis=1)
        for q in (2, 1):
            vals = jnp.where(lanes < 32 * (q + 1), pltpu.roll(part[q], 32 * q, axis=1), vals)
        vals = jnp.where(lanes < 32, part[0], vals)
        meta = jnp.zeros((FORM * 16, 128), f32)
        for q in range(4):
            moved = pltpu.roll(part[q], (96 + 2 * q) % 128, axis=1)
            meta = jnp.where((lanes >= 2 * q) & (lanes < 2 * q + 2), moved, meta)
        for shift in (8, 16, 32, 64):
            meta = meta + pltpu.roll(meta, shift, axis=1)
        meta = jnp.sum(jnp.where(spot, meta, 0.0).reshape(FORM, 16, 128), axis=1)
        to = pl.ds(pl.multiple_of(t * FORM, FORM), FORM)
        msg[to, pl.ds(0, ROWS), :] = vals.reshape(FORM, 16, 128)
        msg[to, pl.ds(ROWS, 1), :] = meta[:, None, :]
        return 0

    lax.fori_loop(0, peers // FORM, form, 0)


def pack(owner, local, coef, stream_t, peers):
    groups = owner.shape[0]
    return pl.pallas_call(
        pack_kernel,
        out_shape=(
            jax.ShapeDtypeStruct((groups, 128), i32),
            jax.ShapeDtypeStruct((peers, MSG, 128), f32),
        ),
        in_specs=[VM] * 4,
        out_specs=(VM, VM),
        scratch_shapes=[
            pltpu.VMEM((groups * 128, 128), f32),
            pltpu.VMEM((peers * CAP, 128), f32),
            pltpu.VMEM((groups, 128), i32),
            pltpu.SMEM((groups, 128), i32),
            pltpu.SemaphoreType.DMA,
        ],
        compiler_params=pltpu.CompilerParams(vmem_limit_bytes=48 << 20),
        name="pack",
    )(owner, local, coef, stream_t)


def flux_of(messages, top, acc, put):
    count = len(messages)
    rows = count * ROWS
    lane = iota((rows, 128), 1)
    lane_f, place, side = lane.astype(f32), lane // 32, (lane // 64).astype(f32)
    vals = jnp.concatenate([m[0:ROWS, :] for m in messages], axis=0)
    meta = jnp.concatenate(
        [
            pltpu.roll(jnp.broadcast_to(m[ROWS : ROWS + 1, :], (ROWS, 128)), 0, axis=1, stride=8, stride_axis=0)
            for m in messages
        ],
        axis=0,
    )

    def by_place(parts):
        out = parts[3]
        for q in (2, 1, 0):
            out = jnp.where(place == q, parts[q], out)
        return out

    onehots, parts, coefs = [], [], []
    for q in range(4):
        column = jnp.broadcast_to(meta[:, 2 * q : 2 * q + 1], (rows, 128))
        part = jnp.floor(column * (1.0 / 256.0))
        low = column - 256.0 * part
        onehots.append(
            jnp.concatenate(
                [jnp.where(low == lane_f + 128.0 * b, 1.0, 0.0).astype(bf16) for b in range(2)], axis=1
            )
        )
        parts.append(part)
        coefs.append(jnp.broadcast_to(meta[:, 2 * q + 1 : 2 * q + 2], (rows, 128)))
    onehot = jnp.concatenate(onehots, axis=0)
    picked = dot(onehot, top[...])
    tops = []
    for q in range(4):
        p = picked[rows * q : rows * q + rows, :]
        p = jnp.where(parts[q] == side, p[:, 0:128], 0.0) + jnp.where(parts[q] == side + 2.0, p[:, 128:256], 0.0)
        p = p + pltpu.roll(p, 64, axis=1)
        tops.append(p + pltpu.roll(p, 32, axis=1))
    flux = by_place(coefs) * (vals - by_place(tops))
    for p in range(count):
        put(p, flux[ROWS * p : ROWS * p + ROWS, :])
    flux_t, part_t = flux.T, by_place(parts).T
    flux_t = jnp.concatenate([flux_t[32 * q : 32 * q + 32, :] for q in range(4)], axis=1)
    part_t = jnp.concatenate([part_t[32 * q : 32 * q + 1, :] for q in range(4)], axis=1)
    high = flux_t.astype(bf16).astype(f32)
    both = jnp.concatenate([high, flux_t - high], axis=0)
    spread = jnp.concatenate([jnp.where(part_t == float(g), both, 0.0).astype(bf16) for g in range(4)], axis=0)
    acc[...] += dot(spread, onehot)


def top_of(state_top, top):
    lane = iota((256, 128), 1)
    quarters = []
    for g in range(4):
        t = jnp.where(lane < 32, state_top[256 * g : 256 * g + 256, :], 0.0)
        high = t.astype(bf16).astype(f32)
        quarters.append(high + pltpu.roll(t - high, 32, axis=1))
    top[...] = jnp.concatenate(
        [quarters[g] + pltpu.roll(quarters[g + 1], 64, axis=1) for g in (0, 2)], axis=1
    ).astype(bf16)


def prepare(st, y_in, lat_col, count, diff, rhs, iface):
    row = iota((32, 128), 0)

    def step(cb, _):
        block, lanes = cb // 2, pl.ds(pl.multiple_of(lax.rem(cb, 2) * 128, 128), 128)
        lats = [jnp.broadcast_to(lat_col[cb, :, x : x + 1], (32, 128)) for x in range(4)]
        for j in range(16):
            at = slice(128 * j, 128 * j + 128)
            parts = []
            for x in range(4):
                here = 4 * cb + x
                s = st[here + 1, :, at]
                lower = jnp.where(row == 0, y_in[0, here, :, at], pltpu.roll(s, 1, axis=0))
                upper = jnp.where(row == 31, y_in[1, here, :, at], pltpu.roll(s, 31, axis=0))
                beside = (st[here, :, at] + st[here + 2, :, at]) + (lower + upper)
                parts.append(s + lats[x] * (beside - 4.0 * s))
            rhs[block, at, lanes] = jnp.concatenate(parts, axis=0).T
        counts = jnp.concatenate([count[pl.ds(4 * cb + x, 1), :] for x in range(4)], axis=1)
        d = diff[pl.ds(4 * cb, 4)].reshape(128, 64)
        d = jnp.concatenate([d, jnp.zeros((128, 64), f32)], axis=1).T[0:64, :]
        iface[block, :, lanes] = jnp.where(iota((64, 128), 0) + 1 < counts, d, 0.0)
        return 0

    lax.fori_loop(0, 8, step, 0)


def eliminate(rhs, coef, iface, scale_col, block):
    scales = jnp.concatenate([scale_col[...]] * 4, axis=1)

    def cell(k):
        return pl.ds(32 * k, 32)

    def put(ref, k, value):
        ref[block, cell(k), :] = value[:, 0:256]
        ref[block + 1, cell(k), :] = value[:, 256:512]

    def get(k):
        return jnp.concatenate([rhs[block, cell(k), :], rhs[block + 1, cell(k), :]], axis=1)

    def layers(n, carry):
        c, d, u = carry
        for m in range(7):
            k = 63 - 7 * n - m
            v = scales * jnp.concatenate([iface[block, pl.ds(k - 1, 1), :], iface[block + 1, pl.ds(k - 1, 1), :]], axis=1)
            r = 1.0 / (1.0 + v + u * (1.0 - c))
            d = (get(k) + u * d) * r
            c = v * r
            u = v
            put(rhs, k, d)
            put(coef, k, c)
        return c, d, u

    zero = jnp.zeros((32, 512), f32)
    c, d, u = lax.fori_loop(0, 9, layers, (zero, zero, zero))
    r = 1.0 / (1.0 + u * (1.0 - c))
    put(rhs, 0, (get(0) + u * d) * r)
    put(coef, 0, r)


PART = 8


def columns_last(a, out):
    a = jnp.concatenate([a, jnp.zeros((32, 96), f32)], axis=1)
    a = jnp.concatenate([a, jnp.zeros((96, 128), f32)], axis=0).T
    for g in range(8):
        out[g] = pltpu.roll(a, (128 - 4 * g) % 128, axis=1)[0:32, :]


def weights_of(left, right, stoich_t, w_a, w_b, s_both, s_high):
    inside = iota((64, 128), 0) // 32 == iota((64, 128), 1) // 64

    def spread(w):
        return jnp.where(inside, jnp.concatenate([jnp.concatenate([w] * 2, axis=1)] * 2, axis=0), 0.0)

    pair = jnp.concatenate([spread(left[...]), spread(right[...])], axis=1)
    high, low = split(pair)
    none = jnp.zeros((64, 256), bf16)
    w_a[...] = jnp.concatenate([high, high, low, none], axis=0)
    w_b[...] = jnp.concatenate([high, high, none, low], axis=0)
    inside = iota((128, 256), 0) // 32 == iota((128, 256), 1) // 64
    wide = jnp.concatenate([stoich_t[...]] * 4, axis=1)
    high, low = split(jnp.where(inside, jnp.concatenate([wide] * 4, axis=0), 0.0).T)
    s_both[...] = jnp.concatenate([high, low], axis=1)
    s_high[...] = high


def finish(rhs, coef, count_col, acc, w_a, w_b, s_both, s_high, solved_t, st, i):
    lane = iota((128, 128), 1)
    at = pl.multiple_of(64 * i, 64)
    source = acc[pl.ds(at, 32), :] + acc[pl.ds(at + 32, 32), :]
    x = rhs[i, 0:32, :] + coef[i, 0:32, :] * source
    solved_t[0:32, :] = x
    for k in range(1, 64):
        cell = slice(32 * k, 32 * k + 32)
        x = rhs[i, cell, :] + coef[i, cell, :] * x
        solved_t[cell, :] = x

    half = lane < 64
    for cb in range(2):
        counts = jnp.concatenate(
            [jnp.broadcast_to(count_col[2 * i + cb, :, x : x + 1], (32, 128)) for x in range(4)], axis=0
        )
        depth = counts - (lane // 32).astype(f32)
        for first in range(0, 16, PART):
            solved, pair_a, pair_b = [], [], []
            for j in range(first, first + PART):
                x = solved_t[128 * j : 128 * j + 128, 128 * cb : 128 * cb + 128].T
                high = x.astype(bf16)
                wide = high.astype(f32)
                low = pltpu.roll(x - wide, 64, axis=1)
                pair_a.append(jnp.concatenate([jnp.where(half, wide, low).astype(bf16), high], axis=1))
                pair_b.append(jnp.concatenate([jnp.where(half, low, wide).astype(bf16), high], axis=1))
                solved.append(x)
            both = dot(jnp.concatenate(pair_a, axis=0), w_a[...])
            rates_a = split(both[:, 0:128] * both[:, 128:256])
            both = dot(jnp.concatenate(pair_b, axis=0), w_b[...])
            rates_b = split(both[:, 0:128] * both[:, 128:256])
            change = dot(jnp.concatenate([rates_a[0], rates_b[0]], axis=1), s_both[...])
            change = change[:, 0:128] + change[:, 128:256]
            change = change + dot(jnp.concatenate([rates_a[1], rates_b[1]], axis=1), s_high[...])
            for n in range(PART):
                j = first + n
                new = solved[n] + jnp.where(depth > 4.0 * j, 0.1, 0.0) * change[128 * n : 128 * n + 128, :]
                for p in range(4):
                    st[8 * i + 4 * cb + p + 1, :, 128 * j : 128 * j + 128] = new[32 * p : 32 * p + 32, :]


def exchange_kernel(
    msg, state, lat, count, diff, scale, left, right, stoich_t, back, done,
    st, y_in, y_out, rhs, coef, iface, lat_col, count_col, scale_col, inbox, outbox, top, acc,
    w_a, w_b, s_both, s_high, solved_t,
    send1, recv1, send2, recv2, send_edge, recv_edge, local,
):
    peers = msg.shape[0]
    size_x, size_y = lax.axis_size("gx"), lax.axis_size("gy")
    gx, gy = lax.axis_index("gx"), lax.axis_index("gy")
    me = gx * size_y + gy
    tile_x, tile_y, _ = state.shape

    def device(t):
        return (t // size_y, lax.rem(t, size_y))

    barrier = pltpu.get_barrier_semaphore()

    def greet(d, _):
        pl.semaphore_signal(barrier, inc=1, device_id=device(lax.rem(me + d, peers)), device_id_type=MESH)
        return 0

    lax.fori_loop(1, peers, greet, 0)
    load = pltpu.make_async_copy(state, st.at[pl.ds(1, tile_x)], local.at[0])
    load.start()

    edges = [
        (state.at[pl.ds(tile_x - 1, 1)], st.at[pl.ds(0, 1)], (lax.rem(gx + 1, size_x), gy), gx < size_x - 1, gx > 0),
        (state.at[pl.ds(0, 1)], st.at[pl.ds(tile_x + 1, 1)], (lax.rem(gx + size_x - 1, size_x), gy), gx > 0, gx < size_x - 1),
        (y_out.at[0], y_in.at[0], (gx, lax.rem(gy + 1, size_y)), gy < size_y - 1, gy > 0),
        (y_out.at[1], y_in.at[1], (gx, lax.rem(gy + size_y - 1, size_y)), gy > 0, gy < size_y - 1),
    ]

    def edge(n):
        block, to, device_id, _, _ = edges[n]
        return pltpu.make_async_remote_copy(
            src_ref=block,
            dst_ref=to,
            send_sem=send_edge.at[n],
            recv_sem=recv_edge.at[n],
            device_id=device_id,
            device_id_type=MESH,
        )

    for n in range(4):
        @pl.when(jnp.logical_not(edges[n][4]))
        def _():
            edges[n][1][...] = jnp.zeros(edges[n][1].shape, f32)

    def send(d):
        to = lax.rem(me + d, peers)
        return pltpu.make_async_remote_copy(
            src_ref=msg.at[to],
            dst_ref=inbox.at[d],
            send_sem=send1,
            recv_sem=recv1.at[d],
            device_id=device(to),
            device_id_type=MESH,
        )

    def reply(d):
        to = lax.rem(me + peers - d, peers)
        return pltpu.make_async_remote_copy(
            src_ref=outbox.at[d],
            dst_ref=back.at[me],
            send_sem=send2,
            recv_sem=recv2,
            device_id=device(to),
            device_id_type=MESH,
        )

    def start(d, _):
        send(d).start()
        return 0

    columns_last(lat[...], lat_col)
    columns_last(count[...].astype(f32), count_col)
    scale_col[...] = jnp.broadcast_to(
        jnp.sum(
            jnp.where(iota((32, 32), 0) == iota((32, 32), 1), jnp.broadcast_to(scale[...], (32, 32)), 0.0),
            axis=1,
            keepdims=True,
        ),
        (32, 128),
    )
    acc[...] = jnp.zeros_like(acc)
    weights_of(left, right, stoich_t, w_a, w_b, s_both, s_high)
    load.wait()

    def gather(x, _):
        y_out[0, x] = st[x + 1, tile_y - 1 : tile_y, :]
        y_out[1, x] = st[x + 1, 0:1, :]
        return 0

    lax.fori_loop(0, tile_x, gather, 0, unroll=4)
    top_of(st[1 : tile_x + 1, :, 0:128].reshape(tile_x * tile_y, 128), top)
    pl.semaphore_wait(barrier, peers - 1)
    for n in range(4):
        pl.when(edges[n][3])(edge(n).start)
    lax.fori_loop(1, peers, start, 0)
    keep = pltpu.make_async_copy(msg.at[me], inbox.at[0], recv1.at[0])
    keep.start()

    for n in range(4):
        pl.when(edges[n][4])(edge(n).wait_recv)
    prepare(st, y_in, lat_col, count, diff, rhs, iface)
    for block in (0, 2):
        eliminate(rhs, coef, iface, scale_col, block)
    keep.wait()

    def work(c, first):
        for p in range(BATCH):
            if not (first and p == 0):
                send(c * BATCH + p).wait_recv()

        def put(p, value):
            outbox[pl.ds(c * BATCH + p, 1)] = value[None]

        flux_of([inbox[c * BATCH + p] for p in range(BATCH)], top, acc, put)
        for p in range(BATCH):
            if not (first and p == 0):
                reply(c * BATCH + p).start()

    work(0, True)

    def step(c, _):
        work(c, False)
        return 0

    lax.fori_loop(1, peers // BATCH, step, 0)
    own = pltpu.make_async_copy(outbox.at[0], back.at[me], recv1.at[0])
    own.start()
    whole = pltpu.make_async_copy(st.at[pl.ds(1, tile_x)], done, local.at[1])

    def columns(i, _):
        finish(rhs, coef, count_col, acc, w_a, w_b, s_both, s_high, solved_t, st, i)
        part = pl.ds(8 * i, 8)
        pltpu.make_async_copy(st.at[pl.ds(8 * i + 1, 8)], done.at[part], local.at[1]).start()
        return 0

    lax.fori_loop(0, tile_x // 8, columns, 0)
    whole.wait()
    own.wait()
    for n in range(4):
        pl.when(edges[n][3])(edge(n).wait_send)
    rest = pl.ds(0, peers - 1)
    pltpu.make_async_copy(msg.at[rest], msg.at[rest], send1).wait()
    pltpu.make_async_copy(outbox.at[rest], outbox.at[rest], send2).wait()
    pltpu.make_async_copy(back.at[rest], back.at[rest], recv2).wait()


def exchange(msg, state, lat, count, diffusion, scale, left, right, stoich_t):
    peers = msg.shape[0]
    tile_x, tile_y, width = state.shape
    return pl.pallas_call(
        exchange_kernel,
        out_shape=(
            jax.ShapeDtypeStruct((peers, ROWS, 128), f32),
            jax.ShapeDtypeStruct(state.shape, f32),
        ),
        in_specs=[ANY, ANY] + [VM] * 7,
        out_specs=(ANY, ANY),
        scratch_shapes=[
            pltpu.VMEM((tile_x + 2, tile_y, width), f32),
            pltpu.VMEM((2, tile_x, 1, width), f32),
            pltpu.VMEM((2, tile_x, 1, width), f32),
            pltpu.VMEM((4, width, 256), f32),
            pltpu.VMEM((4, width, 256), f32),
            pltpu.VMEM((4, 64, 256), f32),
            pltpu.VMEM((8, 32, 128), f32),
            pltpu.VMEM((8, 32, 128), f32),
            pltpu.VMEM((32, 128), f32),
            pltpu.VMEM((peers, MSG, 128), f32),
            pltpu.VMEM((peers, ROWS, 128), f32),
            pltpu.VMEM((256, 256), bf16),
            pltpu.VMEM((256, 256), f32),
            pltpu.VMEM((256, 256), bf16),
            pltpu.VMEM((256, 256), bf16),
            pltpu.VMEM((256, 256), bf16),
            pltpu.VMEM((256, 128), bf16),
            pltpu.VMEM((width, 256), f32),
            pltpu.SemaphoreType.DMA,
            pltpu.SemaphoreType.DMA((peers,)),
            pltpu.SemaphoreType.DMA,
            pltpu.SemaphoreType.DMA,
            pltpu.SemaphoreType.DMA((4,)),
            pltpu.SemaphoreType.DMA((4,)),
            pltpu.SemaphoreType.DMA((2,)),
        ],
        compiler_params=pltpu.CompilerParams(collective_id=0, has_side_effects=True, vmem_limit_bytes=58 << 20),
        name="exchange",
    )(msg, state, lat, count, diffusion, scale, left, right, stoich_t)


def unpack_kernel(flat, back, stream_t, done, out, state_out, buf, rows, held, sem):
    load = pltpu.make_async_copy(done, held, sem.at[0])
    store = pltpu.make_async_copy(held, state_out, sem.at[1])
    load.start()
    groups = flat.shape[0]
    peers = back.shape[0]

    def spread(t, _):
        m = back[pl.ds(pl.multiple_of(t * FORM, FORM), FORM)].reshape(FORM * 16, 128)
        parts = [m] + [pltpu.roll(m, 128 - 32 * q, axis=1) for q in range(1, 4)]
        parts = [p.reshape(FORM, 1, 16, 128) for p in parts]
        at = pl.multiple_of(t * FORM * CAP, FORM * CAP)
        buf[pl.ds(at, FORM * CAP), :] = jnp.concatenate(parts, axis=1).reshape(FORM * CAP, 128)
        return 0

    lax.fori_loop(0, peers // FORM, spread, 0)

    def move(g, _):
        at = pl.multiple_of(g * 128, 128)
        for j in range(128):
            rows[pl.ds(j, 1), :] = buf[pl.ds(flat[g, j], 1), :]
        out[:, pl.ds(at, 128)] = stream_t[:, pl.ds(at, 128)] - 0.5 * rows[...].T[0:32, :]
        return 0

    load.wait()
    store.start()
    lax.fori_loop(0, groups, move, 0)
    store.wait()


def unpack(flat, back, stream_t, done):
    peers = back.shape[0]
    return pl.pallas_call(
        unpack_kernel,
        out_shape=(jax.ShapeDtypeStruct(stream_t.shape, f32), jax.ShapeDtypeStruct(done.shape, f32)),
        in_specs=[pl.BlockSpec(memory_space=pltpu.SMEM), VM, VM, ANY],
        out_specs=(VM, ANY),
        scratch_shapes=[pltpu.VMEM((peers * CAP, 128), f32), pltpu.VMEM((128, 128), f32), pltpu.VMEM(done.shape, f32), pltpu.SemaphoreType.DMA((2,))],
        compiler_params=pltpu.CompilerParams(vmem_limit_bytes=48 << 20),
        name="unpack",
    )(flat, back, stream_t, done)


def body(
    state,
    lat_coef,
    diffusion,
    layer_count,
    species_scale,
    stream,
    reach_owner,
    reach_local,
    exch_coef,
    rate_left,
    rate_right,
    stoich,
):
    peers = lax.axis_size("gx") * lax.axis_size("gy")
    stream_t = stream.T
    flat, msg = pack(
        reach_owner.reshape(-1, 128), reach_local.reshape(-1, 128), exch_coef.reshape(-1, 128), stream_t, peers
    )
    back, done = exchange(
        msg, state, lat_coef, layer_count, diffusion, species_scale[None, :], rate_left, rate_right, stoich.T
    )
    stream_out, state_out = unpack(flat, back, stream_t, done)
    return (state_out, stream_out.T)


def solution(mesh):
    return jax.shard_map(
        body,
        mesh=mesh,
        in_specs=(
            P("gx", "gy", None),
            P("gx", "gy"),
            P("gx", "gy", None),
            P("gx", "gy"),
            P(),
            P(("gx", "gy"), None),
            P(("gx", "gy"), None),
            P(("gx", "gy")),
            P(("gx", "gy")),
            P(),
            P(),
            P(),
        ),
        out_specs=(P("gx", "gy", None), P(("gx", "gy"), None)),
        check_vma=False,
    )
```

time: 106 us -> 95.1 us (0.90); the launches traced: 106 us -> 93.5 us
  Pallas kernels: 101 us -> 87.3 us
  local copies, waits for them, and re-layouts: 4.34 us -> 5.54 us
    pallas_call x3 -> x2, Pallas kernels: 88.6 us -> 74.8 us  [the longest x1 64.2 us: exchange(): pl.pallas_call(exchange_kernel, out_shape=(jax.ShapeDtypeStruct((peers, R...]
    unnamed x14, local copies, waits for them, and re-layouts: 4.34 us -> 5.54 us
where the time goes in v3:
time: 95.1 us; the launch traced here: 93.5 us
  Pallas kernels  87.3 us (92%)
  local copies, waits for them, and re-layouts  5.54 us (6%)
    pallas_call x1, Pallas kernels, exchange(): pl.pallas_call(exchange_kernel, out_shape=(jax.ShapeDtypeStruct((peers, R...  64.2 us
    pallas_call x1, Pallas kernels, pack(): pl.pallas_call(pack_kernel, out_shape=(jax.ShapeDtypeStruct((groups, 128)...  12.5 us
    pallas_call x1, Pallas kernels, unpack(): pl.pallas_call(unpack_kernel, out_shape=(jax.ShapeDtypeStruct(stream_t.sh...  10.6 us
    unnamed x14, local copies, waits for them, and re-layouts  5.54 us

profile of v3, /device:TPU:1, one launch (start us, length us, event | category | flops | bytes accessed | tf_op | source)
XLA Modules:
  0.0 93.5 jit_solution(10129341368935108770)
XLA Ops:
  0.6 0.0 copy-start
  0.6 1.0 %copy-done = f32[4096,32]{0,1:T(8,128)S(1)} copy-done((f32[4096,32]{0,1:T(8,128)S(1)}, f32[4096,32]{0,1:T(8,128)}, u32[]{:S(2)}) %copy-start) | copy-done | bytes 524312
  1.7 0.0 copy-start.4
  1.7 0.7 copy-done.4
  2.4 0.0 copy-start.5
  2.4 0.7 copy-done.5
  3.1 0.0 copy-start.6
  3.1 0.7 copy-done.6
  3.8 0.0 copy-start.1
  3.8 12.5 %pack.1 = (s32[32,128]{1,0:T(8,128)S(1)}, f32[128,17,128]{2,1,0:T(8,128)S(1)}) custom-call(s32[32,128]{1,0:T(8,128)S(1)} %bitcast.9, s32[32,128]{1,0:T(8,128)S(1)} %bitcast.10, f32[32,128]{1,0:T(8,128)S(1)} %bitcast.11, f32[32,4096]{1,0:T(8,128)S(1)} %bitcast.7), custom_call_target="tpu_custom_call" | custom-call | tf_op jit(solution)/shard_map/pack/pallas_call | solution.py:110
  16.4 0.0 copy-start.2
  16.4 1.1 %copy-done.2 = f32[128,17,128]{2,1,0:T(8,128)} copy-done((f32[128,17,128]{2,1,0:T(8,128)}, f32[128,17,128]{2,1,0:T(8,128)S(1)}, u32[]{:S(2)}) %copy-start.2) | copy-done | bytes 1114136
  17.5 64.2 %exchange.1 = (f32[128,16,128]{2,1,0:T(8,128)}, f32[32,32,2048]{2,1,0:T(8,128)}) custom-call(f32[128,17,128]{2,1,0:T(8,128)} %copy-done.2, f32[32,32,2048]{2,1,0:T(8,128)} %state.1, f32[32,32]{1,0:T(8,128)} %lat.1, s32[32,32]{1,0:T(8,128)} %count.1, f32[32,32,64]{2,1,0:T(8,128)} %diff.1, f32[1,32]{1,0:T(1,128)} %bitcast.13, f32[32,64]{1,0:T(8,128)} %left.1, ...), custom_call_target="tpu_custom_call" | custom-call | tf_op jit(solution)/shard_map/exchange/pallas_call | solution.py:475
  81.7 0.0 copy-done.1
  81.7 0.0 copy-start.3
  81.7 1.2 %copy-done.3 = f32[128,16,128]{2,1,0:T(8,128)S(1)} copy-done((f32[128,16,128]{2,1,0:T(8,128)S(1)}, f32[128,16,128]{2,1,0:T(8,128)}, u32[]{:S(2)}) %copy-start.3) | copy-done | bytes 1048600
  82.9 10.6 %unpack.1 = (f32[32,4096]{1,0:T(8,128)}, f32[32,32,2048]{2,1,0:T(8,128)}) custom-call(s32[32,128]{1,0:T(8,128)S(1)} %get-tuple-element.8.flat, f32[128,16,128]{2,1,0:T(8,128)S(1)} %copy-done.3, f32[32,4096]{1,0:T(8,128)S(1)} %bitcast.8, f32[32,32,2048]{2,1,0:T(8,128)} %get-tuple-element.11.done), custom_call_target="tpu_custom_call" | custom-call | tf_op jit(solution)/shard_map/unpack/pallas_call | solution.py:547
Async XLA Ops:
  0.6 1.0 %copy-start = (f32[4096,32]{0,1:T(8,128)S(1)}, f32[4096,32]{0,1:T(8,128)}, u32[]{:S(2)}) copy-start(f32[4096,32]{0,1:T(8,128)} %param.17) | copy-start | bytes 1572868
  1.7 0.7 copy-start.4
  2.4 0.7 copy-start.5
  3.1 0.7 copy-start.6
  3.8 77.9 %copy-start.1 = (f32[4096,32]{0,1:T(8,128)S(1)}, f32[4096,32]{0,1:T(8,128)}, u32[]{:S(2)}) copy-start(f32[4096,32]{0,1:T(8,128)} %param.17) | copy-start | bytes 1572868
  16.4 1.1 %copy-start.2 = (f32[128,17,128]{2,1,0:T(8,128)}, f32[128,17,128]{2,1,0:T(8,128)S(1)}, u32[]{:S(2)}) copy-start(f32[128,17,128]{2,1,0:T(8,128)S(1)} %get-tuple-element.9.msg) | copy-start | bytes 3342340
  81.7 1.2 %copy-start.3 = (f32[128,16,128]{2,1,0:T(8,128)S(1)}, f32[128,16,128]{2,1,0:T(8,128)}, u32[]{:S(2)}) copy-start(f32[128,16,128]{2,1,0:T(8,128)} %get-tuple-element.10.back) | copy-start | bytes 3145732

commit v4 on v3

--- a/solution.py
+++ b/solution.py
@@ -15,8 +15,9 @@
 CAP = 64
 ROWS = 16
 MSG = ROWS + 1
-FORM = 16
+FORM = 32
 BATCH = 16
+STRIDE = 45
 
 
 def iota(shape, dim):
@@ -32,13 +33,21 @@
     return jnp.dot(a, b, preferred_element_type=f32)
 
 
-def pack_kernel(owner, local, coef, stream_t, flat_out, msg, rows, buf, flat_v, flat_s, sem):
+def pack_kernel(
+    owner_in, local_in, coef_in, stream_in, flat_out, msg_out,
+    owner, local, coef, stream_t, msg, rows, buf, flat_v, flat_s, sem,
+):
     groups = owner.shape[0]
     peers = msg.shape[0]
+    inputs = ((owner_in, owner), (local_in, local), (coef_in, coef), (stream_in, stream_t))
+    loads = [pltpu.make_async_copy(a, b, sem.at[n]) for n, (a, b) in enumerate(inputs)]
+    for load in loads:
+        load.start()
     sub, lane = iota((128, 128), 0), iota((128, 128), 1)
     upto = (sub <= lane).astype(bf16)
     ones = jnp.ones((128, 128), bf16)
     carry = jnp.zeros((128, 128), f32)
+    loads[0].wait()
     for g in range(groups):
         mine = sub == owner[g : g + 1, :]
         onehot = mine.astype(f32).astype(bf16)
@@ -46,8 +55,11 @@
         carry = carry + dot(onehot, ones)
         rank = jnp.sum(jnp.where(mine, count, 0.0), axis=0, keepdims=True)
         flat_v[g : g + 1, :] = owner[g : g + 1, :] * CAP + rank.astype(i32) - 1
-    pltpu.make_async_copy(flat_v, flat_s, sem).start()
+    flat_copy = pltpu.make_async_copy(flat_v, flat_s, sem.at[4])
+    flat_copy.start()
     flat_out[...] = flat_v[...]
+    for load in loads[1:]:
+        load.wait()
 
     def fill(g, _):
         at = pl.multiple_of(g * 128, 128)
@@ -63,15 +75,15 @@
         rows[pl.ds(at, 128), :] = block.T
         return 0
 
-    lax.fori_loop(0, groups, fill, 0)
+    lax.fori_loop(0, groups, fill, 0, unroll=4)
     empty = jnp.where(lane == 32, -1.0, 0.0)
 
     def clear(g, _):
         buf[pl.ds(pl.multiple_of(g * 128, 128), 128), :] = empty
         return 0
 
-    lax.fori_loop(0, buf.shape[0] // 128, clear, 0)
-    pltpu.make_async_copy(flat_v, flat_s, sem).wait()
+    lax.fori_loop(0, buf.shape[0] // 128, clear, 0, unroll=4)
+    flat_copy.wait()
 
     def move(g, _):
         for j in range(128):
@@ -80,29 +92,32 @@
 
     lax.fori_loop(0, groups, move, 0)
     lanes = iota((FORM * 16, 128), 1)
+    group, pair = lanes // 32, lanes % 32 < 2
     spot = lanes // 8 == (16 - iota((FORM * 16, 128), 0) % 16) % 16
 
     def form(t, _):
         at = pl.multiple_of(t * FORM * CAP, FORM * CAP)
         part = buf[pl.ds(at, FORM * CAP), :].reshape(FORM, 4, 16, 128)
         part = [part[:, q].reshape(FORM * 16, 128) for q in range(4)]
-        vals = pltpu.roll(part[3], 96, axis=1)
-        for q in (2, 1):
-            vals = jnp.where(lanes < 32 * (q + 1), pltpu.roll(part[q], 32 * q, axis=1), vals)
-        vals = jnp.where(lanes < 32, part[0], vals)
-        meta = jnp.zeros((FORM * 16, 128), f32)
-        for q in range(4):
-            moved = pltpu.roll(part[q], (96 + 2 * q) % 128, axis=1)
-            meta = jnp.where((lanes >= 2 * q) & (lanes < 2 * q + 2), moved, meta)
+        part = [part[0]] + [pltpu.roll(part[q], 32 * q, axis=1) for q in range(1, 4)]
+        vals = part[3]
+        for q in (2, 1, 0):
+            vals = jnp.where(group == q, part[q], vals)
+        even = jnp.where(pair & (group == 1), part[0], 0.0) + jnp.where(pair & (group == 3), part[2], 0.0)
+        odd = jnp.where(pair & (group == 2), part[1], 0.0) + jnp.where(pair & (group == 0), part[3], 0.0)
+        meta = even + pltpu.roll(odd, 98, axis=1)
+        meta = jnp.where(group == 1, meta, 0.0) + pltpu.roll(jnp.where(group == 3, meta, 0.0), 68, axis=1)
         for shift in (8, 16, 32, 64):
             meta = meta + pltpu.roll(meta, shift, axis=1)
         meta = jnp.sum(jnp.where(spot, meta, 0.0).reshape(FORM, 16, 128), axis=1)
         to = pl.ds(pl.multiple_of(t * FORM, FORM), FORM)
         msg[to, pl.ds(0, ROWS), :] = vals.reshape(FORM, 16, 128)
         msg[to, pl.ds(ROWS, 1), :] = meta[:, None, :]
+        pltpu.make_async_copy(msg.at[to], msg_out.at[to], sem.at[5]).start()
         return 0
 
     lax.fori_loop(0, peers // FORM, form, 0)
+    pltpu.make_async_copy(msg, msg_out, sem.at[5]).wait()
 
 
 def pack(owner, local, coef, stream_t, peers):
@@ -113,16 +128,21 @@
             jax.ShapeDtypeStruct((groups, 128), i32),
             jax.ShapeDtypeStruct((peers, MSG, 128), f32),
         ),
-        in_specs=[VM] * 4,
-        out_specs=(VM, VM),
+        in_specs=[ANY] * 4,
+        out_specs=(VM, ANY),
         scratch_shapes=[
+            pltpu.VMEM(owner.shape, i32),
+            pltpu.VMEM(local.shape, i32),
+            pltpu.VMEM(coef.shape, f32),
+            pltpu.VMEM(stream_t.shape, f32),
+            pltpu.VMEM((peers, MSG, 128), f32),
             pltpu.VMEM((groups * 128, 128), f32),
             pltpu.VMEM((peers * CAP, 128), f32),
             pltpu.VMEM((groups, 128), i32),
             pltpu.SMEM((groups, 128), i32),
-            pltpu.SemaphoreType.DMA,
+            pltpu.SemaphoreType.DMA((6,)),
         ],
-        compiler_params=pltpu.CompilerParams(vmem_limit_bytes=48 << 20),
+        compiler_params=pltpu.CompilerParams(vmem_limit_bytes=60 << 20),
         name="pack",
     )(owner, local, coef, stream_t)
 
@@ -191,7 +211,7 @@
     ).astype(bf16)
 
 
-def prepare(st, y_in, lat_col, count, diff, rhs, iface):
+def prepare(st, y_in, lat_col, rhs):
     row = iota((32, 128), 0)
 
     def step(cb, _):
@@ -208,46 +228,69 @@
                 beside = (st[here, :, at] + st[here + 2, :, at]) + (lower + upper)
                 parts.append(s + lats[x] * (beside - 4.0 * s))
             rhs[block, at, lanes] = jnp.concatenate(parts, axis=0).T
-        counts = jnp.concatenate([count[pl.ds(4 * cb + x, 1), :] for x in range(4)], axis=1)
-        d = diff[pl.ds(4 * cb, 4)].reshape(128, 64)
+        return 0
+
+    lax.fori_loop(0, 8, step, 0)
+
+
+def sizes_of(diff, count, iface):
+    for cb in range(8):
+        counts = jnp.concatenate([count[4 * cb + x : 4 * cb + x + 1, :] for x in range(4)], axis=1)
+        d = diff[4 * cb : 4 * cb + 4].reshape(128, 64)
         d = jnp.concatenate([d, jnp.zeros((128, 64), f32)], axis=1).T[0:64, :]
-        iface[block, :, lanes] = jnp.where(iota((64, 128), 0) + 1 < counts, d, 0.0)
-        return 0
-
-    lax.fori_loop(0, 8, step, 0)
-
-
-def eliminate(rhs, coef, iface, scale_col, block):
-    scales = jnp.concatenate([scale_col[...]] * 4, axis=1)
-
-    def cell(k):
-        return pl.ds(32 * k, 32)
-
-    def put(ref, k, value):
-        ref[block, cell(k), :] = value[:, 0:256]
-        ref[block + 1, cell(k), :] = value[:, 256:512]
-
-    def get(k):
-        return jnp.concatenate([rhs[block, cell(k), :], rhs[block + 1, cell(k), :]], axis=1)
-
+        lanes = slice(128 * (cb % 2), 128 * (cb % 2) + 128)
+        iface[cb // 2, :, lanes] = jnp.where(iota((64, 128), 0) + 1 < counts, d, 0.0)
+
+
+def cell(k):
+    return pl.ds(32 * k, 32)
+
+
+def put2(ref, block, k, value):
+    ref[block, cell(k), :] = value[:, 0:256]
+    ref[block + 1, cell(k), :] = value[:, 256:512]
+
+
+def get2(ref, block, k):
+    return jnp.concatenate([ref[block, cell(k), :], ref[block + 1, cell(k), :]], axis=1)
+
+
+def below(iface, scale_col, block, k):
+    row = jnp.concatenate([iface[block, pl.ds(k, 1), :], iface[block + 1, pl.ds(k, 1), :]], axis=1)
+    return jnp.concatenate([scale_col[...]] * 4, axis=1) * row
+
+
+def factor(coef, pivot, iface, scale_col, block, n, carry):
+    c, u = carry
+    for m in range(7):
+        k = 63 - 7 * n - m
+        v = below(iface, scale_col, block, k - 1)
+        r = 1.0 / (1.0 + v + u * (1.0 - c))
+        c = v * r
+        u = v
+        put2(coef, block, k, c)
+        put2(pivot, block, k, r)
+    return c, u
+
+
+def factor_top(coef, block, carry):
+    c, u = carry
+    put2(coef, block, 0, 1.0 / (1.0 + u * (1.0 - c)))
+
+
+def eliminate(rhs, coef, pivot, iface, scale_col, block):
     def layers(n, carry):
-        c, d, u = carry
+        d, u = carry
         for m in range(7):
             k = 63 - 7 * n - m
-            v = scales * jnp.concatenate([iface[block, pl.ds(k - 1, 1), :], iface[block + 1, pl.ds(k - 1, 1), :]], axis=1)
-            r = 1.0 / (1.0 + v + u * (1.0 - c))
-            d = (get(k) + u * d) * r
-            c = v * r
-            u = v
-            put(rhs, k, d)
-            put(coef, k, c)
-        return c, d, u
+            d = (get2(rhs, block, k) + u * d) * get2(pivot, block, k)
+            u = below(iface, scale_col, block, k - 1)
+            put2(rhs, block, k, d)
+        return d, u
 
     zero = jnp.zeros((32, 512), f32)
-    c, d, u = lax.fori_loop(0, 9, layers, (zero, zero, zero))
-    r = 1.0 / (1.0 + u * (1.0 - c))
-    put(rhs, 0, (get(0) + u * d) * r)
-    put(coef, 0, r)
+    d, u = lax.fori_loop(0, 9, layers, (zero, zero))
+    put2(rhs, block, 0, (get2(rhs, block, 0) + u * d) * get2(coef, block, 0))
 
 
 PART = 8
@@ -322,7 +365,7 @@
 def exchange_kernel(
     msg, state, lat, count, diff, scale, left, right, stoich_t, back, done,
     st, y_in, y_out, rhs, coef, iface, lat_col, count_col, scale_col, inbox, outbox, top, acc,
-    w_a, w_b, s_both, s_high, solved_t,
+    w_a, w_b, s_both, s_high, solved_t, pivot,
     send1, recv1, send2, recv2, send_edge, recv_edge, local,
 ):
     peers = msg.shape[0]
@@ -368,7 +411,7 @@
             edges[n][1][...] = jnp.zeros(edges[n][1].shape, f32)
 
     def send(d):
-        to = lax.rem(me + d, peers)
+        to = lax.rem(me + d * STRIDE, peers)
         return pltpu.make_async_remote_copy(
             src_ref=msg.at[to],
             dst_ref=inbox.at[d],
@@ -379,7 +422,7 @@
         )
 
     def reply(d):
-        to = lax.rem(me + peers - d, peers)
+        to = lax.rem(me + (peers - d) * STRIDE, peers)
         return pltpu.make_async_remote_copy(
             src_ref=outbox.at[d],
             dst_ref=back.at[me],
@@ -388,10 +431,6 @@
             device_id=device(to),
             device_id_type=MESH,
         )
-
-    def start(d, _):
-        send(d).start()
-        return 0
 
     columns_last(lat[...], lat_col)
     columns_last(count[...].astype(f32), count_col)
@@ -405,6 +444,7 @@
     )
     acc[...] = jnp.zeros_like(acc)
     weights_of(left, right, stoich_t, w_a, w_b, s_both, s_high)
+    sizes_of(diff, count, iface)
     load.wait()
 
     def gather(x, _):
@@ -417,15 +457,26 @@
     pl.semaphore_wait(barrier, peers - 1)
     for n in range(4):
         pl.when(edges[n][3])(edge(n).start)
-    lax.fori_loop(1, peers, start, 0)
+    steps, zero = 9, jnp.zeros((32, 512), f32)
+    each = (peers - 1) // (2 * steps)
+    for half, block in enumerate((0, 2)):
+
+        def start(n, carry, half=half, block=block):
+            for m in range(each):
+                send(1 + (half * steps + n) * each + m).start()
+            return factor(coef, pivot, iface, scale_col, block, n, carry)
+
+        factor_top(coef, block, lax.fori_loop(0, steps, start, (zero, zero)))
+    for d in range(1 + 2 * steps * each, peers):
+        send(d).start()
     keep = pltpu.make_async_copy(msg.at[me], inbox.at[0], recv1.at[0])
     keep.start()
 
     for n in range(4):
         pl.when(edges[n][4])(edge(n).wait_recv)
-    prepare(st, y_in, lat_col, count, diff, rhs, iface)
+    prepare(st, y_in, lat_col, rhs)
     for block in (0, 2):
-        eliminate(rhs, coef, iface, scale_col, block)
+        eliminate(rhs, coef, pivot, iface, scale_col, block)
     keep.wait()
 
     def work(c, first):
@@ -447,7 +498,7 @@
         work(c, False)
         return 0
 
-    lax.fori_loop(1, peers // BATCH, step, 0)
+    lax.fori_loop(1, peers // BATCH, step, 0, unroll=7)
     own = pltpu.make_async_copy(outbox.at[0], back.at[me], recv1.at[0])
     own.start()
     whole = pltpu.make_async_copy(st.at[pl.ds(1, tile_x)], done, local.at[1])
@@ -499,6 +550,7 @@
             pltpu.VMEM((256, 256), bf16),
             pltpu.VMEM((256, 128), bf16),
             pltpu.VMEM((width, 256), f32),
+            pltpu.VMEM((4, width, 256), f32),
             pltpu.SemaphoreType.DMA,
             pltpu.SemaphoreType.DMA((peers,)),
             pltpu.SemaphoreType.DMA,
@@ -507,14 +559,18 @@
             pltpu.SemaphoreType.DMA((4,)),
             pltpu.SemaphoreType.DMA((2,)),
         ],
-        compiler_params=pltpu.CompilerParams(collective_id=0, has_side_effects=True, vmem_limit_bytes=58 << 20),
+        compiler_params=pltpu.CompilerParams(collective_id=0, has_side_effects=True, vmem_limit_bytes=60 << 20),
         name="exchange",
     )(msg, state, lat, count, diffusion, scale, left, right, stoich_t)
 
 
-def unpack_kernel(flat, back, stream_t, done, out, state_out, buf, rows, held, sem):
+def unpack_kernel(flat, back_in, stream_in, done, out, state_out, back, stream_t, buf, rows, held, sem):
     load = pltpu.make_async_copy(done, held, sem.at[0])
     store = pltpu.make_async_copy(held, state_out, sem.at[1])
+    load_back = pltpu.make_async_copy(back_in, back, sem.at[2])
+    load_stream = pltpu.make_async_copy(stream_in, stream_t, sem.at[3])
+    load_back.start()
+    load_stream.start()
     load.start()
     groups = flat.shape[0]
     peers = back.shape[0]
@@ -527,7 +583,9 @@
         buf[pl.ds(at, FORM * CAP), :] = jnp.concatenate(parts, axis=1).reshape(FORM * CAP, 128)
         return 0
 
+    load_back.wait()
     lax.fori_loop(0, peers // FORM, spread, 0)
+    load_stream.wait()
 
     def move(g, _):
         at = pl.multiple_of(g * 128, 128)
@@ -547,10 +605,17 @@
     return pl.pallas_call(
         unpack_kernel,
         out_shape=(jax.ShapeDtypeStruct(stream_t.shape, f32), jax.ShapeDtypeStruct(done.shape, f32)),
-        in_specs=[pl.BlockSpec(memory_space=pltpu.SMEM), VM, VM, ANY],
+        in_specs=[pl.BlockSpec(memory_space=pltpu.SMEM), ANY, ANY, ANY],
         out_specs=(VM, ANY),
-        scratch_shapes=[pltpu.VMEM((peers * CAP, 128), f32), pltpu.VMEM((128, 128), f32), pltpu.VMEM(done.shape, f32), pltpu.SemaphoreType.DMA((2,))],
-        compiler_params=pltpu.CompilerParams(vmem_limit_bytes=48 << 20),
+        scratch_shapes=[
+            pltpu.VMEM(back.shape, f32),
+            pltpu.VMEM(stream_t.shape, f32),
+            pltpu.VMEM((peers * CAP, 128), f32),
+            pltpu.VMEM((128, 128), f32),
+            pltpu.VMEM(done.shape, f32),
+            pltpu.SemaphoreType.DMA((4,)),
+        ],
+        compiler_params=pltpu.CompilerParams(vmem_limit_bytes=60 << 20),
         name="unpack",
     )(flat, back, stream_t, done)
 

time: 95.1 us -> 83.3 us (0.88); the launches traced: 93.5 us -> 82.9 us
  local copies, waits for them, and re-layouts: 5.54 us -> 0 us
  Pallas kernels: 87.3 us -> 82.1 us
    unnamed x14 -> x0, local copies, waits for them, and re-layouts: 5.54 us -> none
    pallas_call x1, Pallas kernels: 64.2 us -> 60.4 us  [exchange(): pl.pallas_call(exchange_kernel, out_shape=(jax.ShapeDtypeStruct((peers, R...]
    pallas_call x1, Pallas kernels: 12.5 us -> 10.5 us  [pack(): pl.pallas_call(pack_kernel, out_shape=(jax.ShapeDtypeStruct((groups, 128)...]
where the time goes in v4:
time: 83.3 us; the launch traced here: 82.9 us
  Pallas kernels  82.1 us (99%)
    pallas_call x1, Pallas kernels, exchange(): pl.pallas_call(exchange_kernel, out_shape=(jax.ShapeDtypeStruct((peers, R...  60.4 us
    pallas_call x1, Pallas kernels, unpack(): pl.pallas_call(unpack_kernel, out_shape=(jax.ShapeDtypeStruct(stream_t.sh...  11.2 us
    pallas_call x1, Pallas kernels, pack(): pl.pallas_call(pack_kernel, out_shape=(jax.ShapeDtypeStruct((groups, 128)...  10.5 us

profile of v4, /device:TPU:1, one launch (start us, length us, event | category | flops | bytes accessed | tf_op | source)
XLA Modules:
  0.0 82.9 jit_solution(18410677028836390361)
XLA Ops:
  0.6 10.5 %pack.1 = (s32[32,128]{1,0:T(8,128)}, f32[128,17,128]{2,1,0:T(8,128)}) custom-call(s32[32,128]{1,0:T(8,128)} %bitcast.10, s32[32,128]{1,0:T(8,128)} %bitcast.11, f32[32,128]{1,0:T(8,128)} %bitcast.12, f32[32,4096]{1,0:T(8,128)} %bitcast.7), custom_call_target="tpu_custom_call" | custom-call | tf_op jit(solution)/shard_map/pack/pallas_call | solution.py:125
  11.2 60.4 %exchange.1 = (f32[128,16,128]{2,1,0:T(8,128)}, f32[32,32,2048]{2,1,0:T(8,128)}) custom-call(f32[128,17,128]{2,1,0:T(8,128)} %get-tuple-element.9.msg, f32[32,32,2048]{2,1,0:T(8,128)} %state.1, f32[32,32]{1,0:T(8,128)} %lat.1, s32[32,32]{1,0:T(8,128)} %count.1, f32[32,32,64]{2,1,0:T(8,128)} %diff.1, f32[1,32]{1,0:T(1,128)} %bitcast.13, f32[32,64]{1,0:T(8,128)} %left.1, ...), custom_call_target="tpu_custom_call" | custom-call | tf_op jit(solution)/shard_map/exchange/pallas_call | solution.py:526
  71.6 11.2 %unpack.1 = (f32[32,4096]{1,0:T(8,128)}, f32[32,32,2048]{2,1,0:T(8,128)}) custom-call(s32[32,128]{1,0:T(8,128)} %get-tuple-element.8.flat, f32[128,16,128]{2,1,0:T(8,128)} %get-tuple-element.10.back_in, f32[32,4096]{1,0:T(8,128)} %bitcast.8, f32[32,32,2048]{2,1,0:T(8,128)} %get-tuple-element.11.done), custom_call_target="tpu_custom_call" | custom-call | tf_op jit(solution)/shard_map/unpack/pallas_call | solution.py:605

commit v5 on v4

--- a/solution.py
+++ b/solution.py
@@ -16,6 +16,7 @@
 ROWS = 16
 MSG = ROWS + 1
 FORM = 32
+TURN = 8
 BATCH = 16
 STRIDE = 45
 
@@ -588,15 +589,17 @@
     load_stream.wait()
 
     def move(g, _):
-        at = pl.multiple_of(g * 128, 128)
-        for j in range(128):
-            rows[pl.ds(j, 1), :] = buf[pl.ds(flat[g, j], 1), :]
-        out[:, pl.ds(at, 128)] = stream_t[:, pl.ds(at, 128)] - 0.5 * rows[...].T[0:32, :]
+        for n in range(TURN):
+            for j in range(128):
+                rows[pl.ds(128 * n + j, 1), :] = buf[pl.ds(flat[TURN * g + n, j], 1), :]
+        for n in range(TURN):
+            at = pl.multiple_of((TURN * g + n) * 128, 128)
+            out[:, pl.ds(at, 128)] = stream_t[:, pl.ds(at, 128)] - 0.5 * rows[128 * n : 128 * n + 128, :].T[0:32, :]
         return 0
 
     load.wait()
     store.start()
-    lax.fori_loop(0, groups, move, 0)
+    lax.fori_loop(0, groups // TURN, move, 0)
     store.wait()
 
 
@@ -611,7 +614,7 @@
             pltpu.VMEM(back.shape, f32),
             pltpu.VMEM(stream_t.shape, f32),
             pltpu.VMEM((peers * CAP, 128), f32),
-            pltpu.VMEM((128, 128), f32),
+            pltpu.VMEM((TURN * 128, 128), f32),
             pltpu.VMEM(done.shape, f32),
             pltpu.SemaphoreType.DMA((4,)),
         ],

time: 83.3 us -> 81.9 us (0.983)
  Pallas kernels: 82.1 us -> 80.8 us
    pallas_call x1, Pallas kernels: 11.2 us -> 9.87 us  [unpack(): pl.pallas_call(unpack_kernel, out_shape=(jax.ShapeDtypeStruct(stream_t.sh...]
where the time goes in v5:
time: 81.9 us; the launch traced here: 81.6 us
  Pallas kernels  80.8 us (99%)
    pallas_call x1, Pallas kernels, exchange(): pl.pallas_call(exchange_kernel, out_shape=(jax.ShapeDtypeStruct((peers, R...  60.4 us
    pallas_call x1, Pallas kernels, pack(): pl.pallas_call(pack_kernel, out_shape=(jax.ShapeDtypeStruct((groups, 128)...  10.5 us
    pallas_call x1, Pallas kernels, unpack(): pl.pallas_call(unpack_kernel, out_shape=(jax.ShapeDtypeStruct(stream_t.sh...  9.87 us

profile of v5, /device:TPU:1, one launch (start us, length us, event | category | flops | bytes accessed | tf_op | source)
XLA Modules:
  0.0 81.6 jit_solution(6415459877016275311)
XLA Ops:
  0.6 10.5 %pack.1 = (s32[32,128]{1,0:T(8,128)}, f32[128,17,128]{2,1,0:T(8,128)}) custom-call(s32[32,128]{1,0:T(8,128)} %bitcast.10, s32[32,128]{1,0:T(8,128)} %bitcast.11, f32[32,128]{1,0:T(8,128)} %bitcast.12, f32[32,4096]{1,0:T(8,128)} %bitcast.7), custom_call_target="tpu_custom_call" | custom-call | tf_op jit(solution)/shard_map/pack/pallas_call | solution.py:126
  11.2 60.4 %exchange.1 = (f32[128,16,128]{2,1,0:T(8,128)}, f32[32,32,2048]{2,1,0:T(8,128)}) custom-call(f32[128,17,128]{2,1,0:T(8,128)} %get-tuple-element.9.msg, f32[32,32,2048]{2,1,0:T(8,128)} %state.1, f32[32,32]{1,0:T(8,128)} %lat.1, s32[32,32]{1,0:T(8,128)} %count.1, f32[32,32,64]{2,1,0:T(8,128)} %diff.1, f32[1,32]{1,0:T(1,128)} %bitcast.13, f32[32,64]{1,0:T(8,128)} %left.1, ...), custom_call_target="tpu_custom_call" | custom-call | tf_op jit(solution)/shard_map/exchange/pallas_call | solution.py:527
  71.6 9.9 %unpack.1 = (f32[32,4096]{1,0:T(8,128)}, f32[32,32,2048]{2,1,0:T(8,128)}) custom-call(s32[32,128]{1,0:T(8,128)} %get-tuple-element.8.flat, f32[128,16,128]{2,1,0:T(8,128)} %get-tuple-element.10.back_in, f32[32,4096]{1,0:T(8,128)} %bitcast.8, f32[32,32,2048]{2,1,0:T(8,128)} %get-tuple-element.11.done), custom_call_target="tpu_custom_call" | custom-call | tf_op jit(solution)/shard_map/unpack/pallas_call | solution.py:608
